TPU v7x, 128 devices: a whole 4x4x4 slice. The times are simulated.
128 devices in a mesh: dp: 128 (over y, z, x, core).
Axes of the slice: x: 4, y: 4, z: 4, core: 2. Of those that a mesh axis runs over, the one named last changes fastest.
Arguments:
- params: float32 [16252928], P('dp'), may hold values from -6 to 6
- first_moment: float32 [16252928], P('dp'), may hold values from -2 to 2
- second_moment: float32 [16252928], P('dp'), may hold values from 0.01 to 1
- grads: bfloat16 [16252928], P('dp'), may hold values from -6 to 6
- old_bounds: int32 [129], replicated, may hold values from 0 to 15728640, as said below
- new_bounds: int32 [129], replicated, may hold values from 0 to 15728640, as said below
- seg_start: int32 [64], replicated, may hold values from 0 to 15728576, as said below
Outputs:
- new_params: float32 [16252928], P('dp')
- new_first: float32 [16252928], P('dp')
- new_second: float32 [16252928], P('dp')
Inputs may be any that keep to these rules, and one draw needn't show every extreme that they name: `old_bounds`: starts at 0 and ends at 15728640; every shard holds between 118784 and 126976 elements, exactly 126976 in some shard. `new_bounds`: starts at 0 and ends at 15728640; every shard holds between 118784 and 126976 elements, exactly 126976 in some shard; each entry differs from the same entry of old_bounds by at most 4096, by exactly 4096 somewhere. `seg_start`: strictly rising, the first is 0, all are multiples of 64.
All inputs are finite; a program needn't handle non-finite values.
Results may differ from a plain program's by a relative error of at most 0.0003.
Values sent between devices are 32-bit elements; how exact they have to be, the bound alone decides.
No kernel may reach another device: no remote copies, remote signals or barrier semaphores. Data moves between devices by JAX's collectives and lax.ppermute only.
A program may use at most 64 MiB of HBM per device.

v0:
```python
import jax
import jax.numpy as jnp
from jax import lax
from jax.sharding import Mesh
from jax.sharding import PartitionSpec as P

MARGIN = 4096
SEGS = 64
DP = ("dp_0", "dp_1", "dp_2", "dp_3")


BETA_ONE = 0.9
BETA_TWO = 0.999
CORR_ONE = 1.0 - 0.9**10
CORR_TWO = 1.0 - 0.999**10
DECAY = 0.01
LEARN = 0.1
EPSILON = 1e-06


def over_axes(value, axes):
    for axis in axes:
        value = lax.psum(value, axis)
    return value


def shifted(value, axis, steps):
    count = lax.axis_size(axis)
    leading, last = (max(0, -steps), min(count, count - steps))
    return lax.ppermute(value, axis, [(source, source + steps) for source in range(leading, last)])


def shards(params, first_moment, second_moment, grads, old_bounds, new_bounds, seg_start):
    cap = params.shape[0]
    margin = MARGIN
    device = lax.axis_index(DP)
    old_low = old_bounds[device]
    old_count = old_bounds[device + 1] - old_low
    slots = jnp.arange(cap, dtype=jnp.int32)
    live = slots < old_count
    gradient = grads.astype(jnp.float32)
    moment_new = BETA_ONE * first_moment + (1.0 - BETA_ONE) * gradient
    second_new = BETA_TWO * second_moment + (1.0 - BETA_TWO) * gradient * gradient
    update = moment_new / CORR_ONE / (jnp.sqrt(second_new / CORR_TWO) + EPSILON) + DECAY * params
    position = old_low + slots
    segment = jnp.sum((position[:, None] >= seg_start[None, :]).astype(jnp.int32), axis=1) - 1
    labels = jnp.arange(SEGS, dtype=jnp.int32)
    member = (segment[:, None] == labels[None, :]) & live[:, None]
    weight_part = jnp.sum(jnp.where(member, (params * params)[:, None], 0.0), axis=0)
    update_part = jnp.sum(jnp.where(member, (update * update)[:, None], 0.0), axis=0)
    sums = over_axes(jnp.stack([weight_part, update_part]), DP)
    ratio = jnp.sqrt(sums[0]) / (jnp.sqrt(sums[1]) + EPSILON)
    element_ratio = jnp.sum(
        jnp.where(segment[:, None] == labels[None, :], ratio[None, :], 0.0), axis=1
    )
    weight_new = params - LEARN * element_ratio * update
    state = jnp.where(live[None, :], jnp.stack([weight_new, moment_new, second_new]), 0.0)
    tail = lax.dynamic_slice_in_dim(state, old_count - margin, margin, 1)
    left_rim = shifted(tail, DP, 1)
    right_rim = shifted(state[:, :margin], DP, -1)
    extended = jnp.concatenate([left_rim, state, jnp.zeros((3, margin), jnp.float32)], axis=1)
    extended = lax.dynamic_update_slice_in_dim(extended, right_rim, margin + old_count, 1)
    new_low = new_bounds[device]
    new_count = new_bounds[device + 1] - new_low
    offset = new_low - old_low + margin
    placed = lax.dynamic_slice_in_dim(extended, offset, cap, 1)
    placed = jnp.where((slots < new_count)[None, :], placed, 0.0)
    return (placed[0], placed[1], placed[2])


def solution(mesh):
    torus = Mesh(mesh.devices.reshape(4, 4, 4, 2), ("dp_0", "dp_1", "dp_2", "dp_3"))
    return jax.shard_map(
        shards,
        mesh=torus,
        in_specs=(P(DP), P(DP), P(DP), P(DP), P(), P(), P()),
        out_specs=(P(DP), P(DP), P(DP)),
        check_vma=False,
    )
```

profile of v0, /device:TPU:8, one launch (start us, length us, event | category | flops | bytes accessed | tf_op | source)
XLA Modules:
  0.0 80.9 jit_solution(4468898574828517191)
XLA Ops:
  0.6 0.0 copy-start.3
  0.6 0.0 copy-start
  0.7 1.5 %fusion.9 = (s32[1]{0:T(128)}, s32[1]{0:T(128)}, s32[1]{0:T(128)}, s32[1]{0:T(128)}) fusion(s32[129]{0:T(256)} %param.12, s32[]{:T(128)S(6)} %select_n.35, s32[]{:T(128)S(6)} %select_n.36, s32[129]{0:T(256)} %param.11), kind=kLoop, calls=%fused_computation.26 | loop fusion | bytes 40 | tf_op jit(solution)/shard_map/dynamic_slice | solution.py:64
  2.1 0.7 iota_add_fusion
  4.2 0.0 copy-start.1
  4.2 0.0 copy-start.2
  4.2 0.1 iota_compare_fusion.1
  4.3 4.7 %convert_reduce_fusion = s32[126976]{0:T(1024)S(1)} fusion(s32[126976]{0:T(1024)S(1)} %iota_add_fusion, s32[64]{0:T(128)} %param.13), kind=kLoop, calls=%fused_computation.5 | loop fusion | flops 24252416 | bytes 1016064 | tf_op jit(solution)/shard_map/reduce_sum | solution.py:46
  9.1 0.0 copy-done.3
  9.1 0.0 copy-done
  9.1 0.0 copy-done.1
  9.1 0.0 copy-done.2
  9.1 0.4 fusion.4
  9.5 9.1 %select_reduce_fusion.2 = (f32[64]{0:T(128)S(1)}, f32[64]{0:T(128)S(1)}) fusion(f32[126976]{0:T(1024)S(1)} %get-tuple-element.13, s32[126976]{0:T(1024)S(1)} %broadcast_add_fusion, pred[126976]{0:T(1024)(128)(4,1)S(1)} %iota_compare_fusion.1, f32[126976]{0:T(1024)S(1)} %get-tuple-element.5), kind=kLoop, calls=%fused_computation.2 | loop fusion | flops 48758656 | bytes 1651200 | tf_op jit(solution)/shard_map/reduce_sum | solution.py:49
  18.7 8.7 %psum.28 = f32[2,64]{1,0:T(2,128)S(1)} all-reduce(f32[2,64]{1,0:T(2,128)S(1)} %pad_maximum_fusion), channel_id=1, replica_groups=mesh['dp_0'=4,'dp_1'=4,'dp_2'=4,'dp_3'=2] {'dp_0'}, use_global_device_ids=true, to_apply=%region_3.4 | all-reduce | flops 128 | bytes 1024 | tf_op jit(solution)/shard_map/psum | solution.py:23
  27.4 11.8 %psum.29 = f32[2,64]{1,0:T(2,128)S(1)} all-reduce(f32[2,64]{1,0:T(2,128)S(1)} %psum.28), channel_id=1, replica_groups=mesh['dp_0'=4,'dp_1'=4,'dp_2'=4,'dp_3'=2] {'dp_1'}, use_global_device_ids=true, to_apply=%region_4.5 | all-reduce | flops 128 | bytes 1024 | tf_op jit(solution)/shard_map/psum | solution.py:23
  39.2 10.5 %psum.30 = f32[2,64]{1,0:T(2,128)S(1)} all-reduce(f32[2,64]{1,0:T(2,128)S(1)} %psum.29), channel_id=1, replica_groups=mesh['dp_0'=4,'dp_1'=4,'dp_2'=4,'dp_3'=2] {'dp_2'}, use_global_device_ids=true, to_apply=%region_5.6 | all-reduce | flops 128 | bytes 1024 | tf_op jit(solution)/shard_map/psum | solution.py:23
  49.6 2.6 %psum.31 = f32[2,64]{1,0:T(2,128)S(1)} all-reduce(f32[2,64]{1,0:T(2,128)S(1)} %psum.30), channel_id=1, replica_groups=mesh['dp_0'=4,'dp_1'=4,'dp_2'=4,'dp_3'=2] {'dp_3'}, use_global_device_ids=true, to_apply=%region_6.7 | all-reduce | flops 128 | bytes 1024 | tf_op jit(solution)/shard_map/psum | solution.py:23
  52.3 5.1 %select_reduce_fusion = f32[126976]{0:T(1024)S(1)} fusion(f32[64]{0:T(128)S(1)} %fusion.3, s32[126976]{0:T(1024)S(1)} %broadcast_add_fusion), kind=kLoop, calls=%fused_computation | loop fusion | flops 24252416 | bytes 1016064 | tf_op jit(solution)/shard_map/reduce_sum | solution.py:53
  57.4 0.3 multiply_subtract_fusion
  57.7 1.8 %maximum_select_fusion = f32[3,126976]{1,0:T(4,128)S(1)} fusion(f32[1,126976]{1,0:T(1,128)S(1)} %bitcast.15, f32[1,126976]{1,0:T(1,128)S(1)} %bitcast.14, f32[1,126976]{1,0:T(1,128)S(1)} %bitcast.16, pred[126976]{0:T(1024)(128)(4,1)S(1)} %iota_compare_fusion.1), kind=kLoop, calls=%fused_computation.7 | loop fusion | flops 1142784 | bytes 3174400 | tf_op jit(solution)/shard_map/jit(_where)/select_n | solution.py:57
  59.5 0.1 fusion.8
  59.6 2.1 %collective-permute-start = (f32[3,4096]{1,0:T(4,128)S(1)}, f32[3,4096]{1,0:T(4,128)S(1)}, u32[]{:S(2)}, u32[]{:S(2)}) collective-permute-start(f32[3,4096]{1,0:T(4,128)S(1)} %get-tuple-element.12), channel_id=1, source_target_pairs={{0,1},{1,2},{2,3},{3,4},{4,5},{5,6},{6,7},{7,8},{8,9},{9,10},{10,1... | collective-permute-start | bytes 147464 | tf_op jit(solution)/shard_map/ppermute | solution.py:30
  61.7 7.7 %collective-permute-start.1 = (f32[3,4096]{1,0:T(4,128)S(1)}, f32[3,4096]{1,0:T(4,128)S(1)}, u32[]{:S(2)}, u32[]{:S(2)}) collective-permute-start(f32[3,4096]{1,0:T(4,128)S(1)} %get-tuple-element.11), channel_id=1, source_target_pairs={{1,0},{2,1},{3,2},{4,3},{5,4},{6,5},{7,6},{8,7},{9,8},{10,9},{11,1... | collective-permute-start | bytes 147464 | tf_op jit(solution)/shard_map/ppermute | solution.py:30
  70.7 0.1 iota_compare_fusion.2
  72.1 0.0 collective-permute-done
  72.1 2.0 %maximum_maximum_fusion = f32[3,135168]{1,0:T(4,128)} fusion(f32[3,126976]{1,0:T(4,128)S(1)} %maximum_select_fusion, f32[3,4096]{1,0:T(4,128)S(1)} %collective-permute-done, f32[135168]{0:T(1024)S(1)} %pad.2.clone), kind=kLoop, calls=%fused_computation.6 | loop fusion | flops 811008 | bytes 3735552 | tf_op jit(solution)/shard_map/concatenate | solution.py:61
  74.2 0.0 collective-permute-done.1
  74.2 1.8 %dynamic_update_slice.3 = f32[3,135168]{1,0:T(4,128)} dynamic-update-slice(f32[3,135168]{1,0:T(4,128)} %maximum_maximum_fusion, f32[3,4096]{1,0:T(4,128)S(1)} %collective-permute-done.1, s32[]{:T(128)} %constant.20.clone.1, s32[]{:T(128)S(6)} %select_n.42) | dynamic-update-slice | bytes 98308 | tf_op jit(solution)/shard_map/dynamic_update_slice | solution.py:62
  76.0 2.7 %dynamic-slice_select_fusion = f32[3,126976]{1,0:T(4,128)S(1)} fusion(f32[3,135168]{1,0:T(4,128)} %dynamic_update_slice.3, s32[]{:T(128)S(6)} %select_n.43, pred[126976]{0:T(1024)(128)(4,1)S(1)} %iota_compare_fusion.2), kind=kLoop, calls=%fused_computation.8 | loop fusion | flops 380928 | bytes 3174404 | tf_op jit(solution)/shard_map/jit(_where)/select_n | solution.py:67
  78.7 2.3 %fusion.7 = (f32[1,126976]{1,0:T(1,128)}, f32[1,126976]{1,0:T(1,128)}, f32[1,126976]{1,0:T(1,128)}) fusion(f32[3,126976]{1,0:T(4,128)S(1)} %dynamic-slice_select_fusion), kind=kLoop, calls=%fused_computation.24 | loop fusion | bytes 3047424 | tf_op jit(solution)/shard_map/slice | solution.py:68
  (5 shorter events, 0.1 us)
Async XLA Ops:
  0.6 8.4 %copy-start.3 = (bf16[126976]{0:T(1024)(128)(2,1)S(1)}, bf16[126976]{0:T(1024)(128)(2,1)}, u32[]{:S(2)}) copy-start(bf16[126976]{0:T(1024)(128)(2,1)} %param.10) | copy-start | bytes 761860
  0.6 8.4 %copy-start = (f32[126976]{0:T(1024)S(1)}, f32[126976]{0:T(1024)}, u32[]{:S(2)}) copy-start(f32[126976]{0:T(1024)} %param.7) | copy-start | bytes 1523716
  4.2 4.9 %copy-start.1 = (f32[126976]{0:T(1024)S(1)}, f32[126976]{0:T(1024)}, u32[]{:S(2)}) copy-start(f32[126976]{0:T(1024)} %param.8) | copy-start | bytes 1523716
  4.2 4.9 %copy-start.2 = (f32[126976]{0:T(1024)S(1)}, f32[126976]{0:T(1024)}, u32[]{:S(2)}) copy-start(f32[126976]{0:T(1024)} %param.9) | copy-start | bytes 1523716
  59.6 12.6 %collective-permute-start = (f32[3,4096]{1,0:T(4,128)S(1)}, f32[3,4096]{1,0:T(4,128)S(1)}, u32[]{:S(2)}, u32[]{:S(2)}) collective-permute-start(f32[3,4096]{1,0:T(4,128)S(1)} %get-tuple-element.12), channel_id=1, source_target_pairs={{0,1},{1,2},{2,3},{3,4},{4,5},{5,6},{6,7},{7,8},{8,9},{9,10},{10,1... | collective-permute-start | bytes 147464 | tf_op jit(solution)/shard_map/ppermute | solution.py:30
  61.7 12.5 %collective-permute-start.1 = (f32[3,4096]{1,0:T(4,128)S(1)}, f32[3,4096]{1,0:T(4,128)S(1)}, u32[]{:S(2)}, u32[]{:S(2)}) collective-permute-start(f32[3,4096]{1,0:T(4,128)S(1)} %get-tuple-element.11), channel_id=1, source_target_pairs={{1,0},{2,1},{3,2},{4,3},{5,4},{6,5},{7,6},{8,7},{9,8},{10,9},{11,1... | collective-permute-start | bytes 147464 | tf_op jit(solution)/shard_map/ppermute | solution.py:30
where the time goes:
time: 81.3 us; the launch traced here: 80.9 us
  blocking collectives  33.6 us (41%)
  other arithmetic  27.1 us (33%)
  starting transfers between devices  9.78 us (12%)
  local copies, waits for them, and re-layouts  5.73 us (7%)
  between operations  4.79 us (6%)
    psum x4, blocking collectives, over_axes(): value = lax.psum(value, axis)  33.6 us
    ppermute x2, starting transfers between devices, shifted(): lax.ppermute(value, axis, [(source, source + steps) for source in range(l...  9.78 us
    reduce_sum x1, other arithmetic, shards(): jnp.sum(jnp.where(member, (params * params)[:, None], 0.0), axis=0)  9.14 us
    reduce_sum x1, other arithmetic, shards(): jnp.sum(jnp.where(segment[:, None] == labels[None, :], ratio[None, :], 0....  5.1 us
    reduce_sum x1, other arithmetic, shards(): jnp.sum((position[:, None] >= seg_start[None, :]).astype(jnp.int32), axis=1)  4.75 us
    select_n x1, other arithmetic, shards(): placed = jnp.where((slots < new_count)[None, :], placed, 0.0)  2.68 us
    slice x1, local copies, waits for them, and re-layouts, shards(): return (placed[0], placed[1], placed[2])  2.26 us
    concatenate x1, other arithmetic, shards(): jnp.concatenate([left_rim, state, jnp.zeros((3, margin), jnp.float32)], a...  2.01 us
  transfers between devices with their start and end apart: 2, of which 0 were waited for; matrix products, arithmetic and copies ran while one was open for 3% of the time, Pallas kernels for 0%

commit v1 on v0

v1 whole, which is shorter than its diff:
```python
import jax
import jax.numpy as jnp
from jax import lax
from jax.experimental import pallas as pl
from jax.experimental.pallas import tpu as pltpu
from jax.sharding import PartitionSpec as P

MARGIN = 4096
SEGS = 64
N_DP = 128
LANES = 128
ROWS = 992
RIM = MARGIN // LANES
PAD_ROWS = 1032

BETA_ONE = 0.9
BETA_TWO = 0.999
CORR_ONE = 1.0 - 0.9**10
CORR_TWO = 1.0 - 0.999**10
DECAY = 0.01
LEARN = 0.1
EPSILON = 1e-06

BLOCK = 32
BLOCK_ELEMS = BLOCK * LANES


def lanes_of(rows):
    return lax.broadcasted_iota(jnp.int32, (rows, LANES), 1)


def index_of(rows):
    return lax.broadcasted_iota(jnp.int32, (rows, LANES), 0) * LANES + lanes_of(rows)


def segment_range(seg, low, high):
    first = jnp.int32(-1)
    last = jnp.int32(-1)
    for s in range(SEGS):
        start = seg[s]
        first = first + jnp.where(start <= low, 1, 0)
        last = last + jnp.where(start < high, 1, 0)
    return first, last


def segment_span(seg, s, low, high):
    begin = jnp.maximum(seg[s], low) - low
    following = jnp.where(s == SEGS - 1, high, seg[jnp.minimum(s + 1, SEGS - 1)])
    end = jnp.minimum(following, high) - low
    return begin, end


def prepare(w_hbm, m_hbm, v_hbm, g_hbm, old, seg, pay, w_own, m_own, v_own, u_own, send_core, send_next, m_in, v_in, g_in, sems):
    copies = [
        pltpu.make_async_copy(w_hbm, w_own.at[pl.ds(0, ROWS)], sems.at[0]),
        pltpu.make_async_copy(m_hbm, m_in, sems.at[1]),
        pltpu.make_async_copy(v_hbm, v_in, sems.at[2]),
        pltpu.make_async_copy(g_hbm, g_in, sems.at[3]),
    ]
    for copy in copies:
        copy.start()
    device = lax.axis_index("dp")
    low = old[device]
    high = old[device + 1]
    count = high - low
    first, last = segment_range(seg, low, high)
    for copy in copies:
        copy.wait()

    def update(b, carry):
        rows = pl.ds(pl.multiple_of(b * BLOCK, BLOCK), BLOCK)
        grad = g_in[rows, :].astype(jnp.float32)
        weight = w_own[rows, :]
        moment = BETA_ONE * m_in[rows, :] + (1.0 - BETA_ONE) * grad
        second = BETA_TWO * v_in[rows, :] + (1.0 - BETA_TWO) * grad * grad
        step = moment / CORR_ONE / (jnp.sqrt(second / CORR_TWO) + EPSILON) + DECAY * weight
        m_own[rows, :] = moment
        v_own[rows, :] = second
        u_own[rows, :] = step
        return carry

    lax.fori_loop(0, ROWS // BLOCK, update, 0)

    cut = count - MARGIN
    cut_row = cut // LANES
    cut_lane = lax.rem(cut, LANES)
    back = lax.rem(LANES - cut_lane, LANES)
    even = lax.rem(device, 2) == 0

    def write_rims(head, tail):
        for a, source in enumerate((w_own, m_own, v_own, u_own)):
            head[a] = source[pl.ds(0, RIM), :]
            here = source[pl.ds(cut_row, RIM), :]
            below = source[pl.ds(cut_row + 1, RIM), :]
            tail[a] = pltpu.roll(jnp.where(lanes_of(RIM) >= cut_lane, here, below), back, 1)

    @pl.when(even)
    def _():
        write_rims(send_next, send_core)

    @pl.when(jnp.logical_not(even))
    def _():
        write_rims(send_core, send_next)

    element = index_of(BLOCK)
    lane = lanes_of(8)

    def fold(x):
        return x[0:8] + x[8:16] + x[16:24] + x[24:32]

    def segment(s, packed):
        begin, end = segment_span(seg, s, low, high)

        def add(b, sums):
            weight_sum, update_sum = sums
            rows = pl.ds(pl.multiple_of(b * BLOCK, BLOCK), BLOCK)
            place = element + b * BLOCK_ELEMS
            inside = (place >= begin) & (place < end)
            weight = w_own[rows, :]
            step = u_own[rows, :]
            weight_sum = weight_sum + fold(jnp.where(inside, weight * weight, 0.0))
            update_sum = update_sum + fold(jnp.where(inside, step * step, 0.0))
            return weight_sum, update_sum

        zero = jnp.zeros((8, LANES), jnp.float32)
        weight_sum, update_sum = lax.fori_loop(
            begin // BLOCK_ELEMS, (end + BLOCK_ELEMS - 1) // BLOCK_ELEMS, add, (zero, zero)
        )
        weight_sum = jnp.sum(weight_sum)
        update_sum = jnp.sum(update_sum)
        return packed + jnp.where(lane == s, weight_sum, 0.0) + jnp.where(lane == SEGS + s, update_sum, 0.0)

    packed = lax.fori_loop(first, last + 1, segment, jnp.zeros((8, LANES), jnp.float32))
    for row in range(0, N_DP, 8):
        pay[pl.ds(row, 8), :] = packed


def finish(parts, w_own, m_own, v_own, u_own, from_core, from_next, old, new, seg, w_out, m_out, v_out,
           w_new, m_new, v_new, u_new, heads, rims, sems):
    device = lax.axis_index("dp")
    old_low = old[device]
    old_high = old[device + 1]
    low = new[device]
    high = new[device + 1]
    count = high - low
    shift = low - old_low + MARGIN
    shift_row = shift // LANES
    shift_lane = lax.rem(shift, LANES)
    back = lax.rem(LANES - shift_lane, LANES)
    even = lax.rem(device, 2) == 0
    owns = (w_own, m_own, v_own, u_own)
    news = (w_new, m_new, v_new, u_new)

    def split_rims(left, right):
        for a in range(4):
            heads[a, pl.ds(0, RIM), :] = left[a]
            rims[a, pl.ds(8, RIM), :] = right[a]

    @pl.when(even)
    def _():
        split_rims(from_next, from_core)

    @pl.when(jnp.logical_not(even))
    def _():
        split_rims(from_core, from_next)

    for a in range(4):
        heads[a, pl.ds(RIM, 72), :] = owns[a][pl.ds(0, 72), :]

    element = index_of(BLOCK)
    keep = lanes_of(BLOCK) >= shift_lane

    def moved(here, below, live):
        return jnp.where(live, pltpu.roll(jnp.where(keep, here, below), back, 1), 0.0)

    for a in range(4):
        here = heads[a, pl.ds(shift_row, BLOCK), :]
        below = heads[a, pl.ds(shift_row + 1, BLOCK), :]
        news[a][pl.ds(0, BLOCK), :] = moved(here, below, element < count)

    def move(b, carry):
        live = element + b * BLOCK_ELEMS < count
        source = b * BLOCK + shift_row - RIM
        rows = pl.ds(pl.multiple_of(b * BLOCK, BLOCK), BLOCK)
        for a in range(4):
            here = owns[a][pl.ds(source, BLOCK), :]
            below = owns[a][pl.ds(source + 1, BLOCK), :]
            news[a][rows, :] = moved(here, below, live)
        return carry

    lax.fori_loop(1, ROWS // BLOCK, move, 0)

    cut = old_high - low

    @pl.when(cut < count)
    def _():
        cut_row = cut // LANES
        cut_lane = lax.rem(cut, LANES)
        place = index_of(40) + cut_row * LANES
        taken = (place >= cut) & (place < count)
        fits = lanes_of(40) < LANES - cut_lane
        for a in range(4):
            here = rims[a, pl.ds(8, 40), :]
            above = rims[a, pl.ds(7, 40), :]
            incoming = pltpu.roll(jnp.where(fits, here, above), cut_lane, 1)
            rows = pl.ds(cut_row, 40)
            news[a][rows, :] = jnp.where(taken, incoming, news[a][rows, :])

    m_copy = pltpu.make_async_copy(m_new.at[pl.ds(0, ROWS)], m_out, sems.at[0])
    v_copy = pltpu.make_async_copy(v_new.at[pl.ds(0, ROWS)], v_out, sems.at[1])
    m_copy.start()
    v_copy.start()

    sums = jnp.broadcast_to(jnp.sum(parts[...], axis=0, keepdims=True), (8, LANES))
    ratio = jnp.sqrt(sums) / (jnp.sqrt(pltpu.roll(sums, SEGS, 1)) + EPSILON)
    lane = lanes_of(8)
    first, last = segment_range(seg, low, high)

    def segment(s, carry):
        begin, end = segment_span(seg, s, low, high)
        rate = LEARN * jnp.sum(jnp.where(lane == s, ratio, 0.0), axis=1, keepdims=True)[0:1]

        def apply(b, inner):
            rows = pl.ds(pl.multiple_of(b * BLOCK, BLOCK), BLOCK)
            place = element + b * BLOCK_ELEMS
            inside = (place >= begin) & (place < end)
            weight = w_new[rows, :]
            w_new[rows, :] = jnp.where(inside, weight - rate * u_new[rows, :], weight)
            return inner

        lax.fori_loop(begin // BLOCK_ELEMS, (end + BLOCK_ELEMS - 1) // BLOCK_ELEMS, apply, 0)
        return carry

    lax.fori_loop(first, last + 1, segment, 0)
    w_copy = pltpu.make_async_copy(w_new.at[pl.ds(0, ROWS)], w_out, sems.at[2])
    w_copy.start()
    m_copy.wait()
    v_copy.wait()
    w_copy.wait()


def shards(params, first_moment, second_moment, grads, old_bounds, new_bounds, seg_start):
    any_space = pl.BlockSpec(memory_space=pl.ANY)
    vmem = pl.BlockSpec(memory_space=pltpu.VMEM)
    smem = pl.BlockSpec(memory_space=pltpu.SMEM)
    f32 = jnp.float32
    own = jax.ShapeDtypeStruct((PAD_ROWS, LANES), f32)
    rim = jax.ShapeDtypeStruct((4, RIM, LANES), f32)
    state = pltpu.VMEM((ROWS, LANES), f32)
    flat = [x.reshape(ROWS, LANES) for x in (params, first_moment, second_moment, grads)]
    pay, w_own, m_own, v_own, u_own, send_core, send_next = pl.pallas_call(
        prepare,
        out_shape=(jax.ShapeDtypeStruct((N_DP, LANES), f32), own, own, own, own, rim, rim),
        in_specs=[any_space] * 4 + [smem] * 2,
        out_specs=[vmem] * 7,
        scratch_shapes=[state, state, pltpu.VMEM((ROWS, LANES), jnp.bfloat16), pltpu.SemaphoreType.DMA((4,))],
        compiler_params=pltpu.CompilerParams(vmem_limit_bytes=24 * 2**20),
    )(*flat, old_bounds, seg_start)
    pairs = [(i, i ^ 1) for i in range(N_DP)]
    between = [(i, i + 1) for i in range(1, N_DP - 1, 2)]
    between = between + [(j, i) for i, j in between]
    from_core = lax.ppermute(send_core, "dp", pairs)
    from_next = lax.ppermute(send_next, "dp", between)
    parts = lax.all_to_all(pay, "dp", 0, 0, tiled=True)
    padded = pltpu.VMEM((PAD_ROWS, LANES), f32)
    outs = pl.pallas_call(
        finish,
        out_shape=(jax.ShapeDtypeStruct((ROWS, LANES), f32),) * 3,
        in_specs=[vmem] * 7 + [smem] * 3,
        out_specs=[any_space] * 3,
        scratch_shapes=[padded] * 4
        + [pltpu.VMEM((4, 104, LANES), f32), pltpu.VMEM((4, 48, LANES), f32), pltpu.SemaphoreType.DMA((3,))],
        compiler_params=pltpu.CompilerParams(vmem_limit_bytes=24 * 2**20),
    )(parts, w_own, m_own, v_own, u_own, from_core, from_next, old_bounds, new_bounds, seg_start)
    return tuple(x.reshape(-1) for x in outs)


def solution(mesh):
    return jax.shard_map(
        shards,
        mesh=mesh,
        in_specs=(P("dp"), P("dp"), P("dp"), P("dp"), P(), P(), P()),
        out_specs=(P("dp"), P("dp"), P("dp")),
        check_vma=False,
    )
```

time: 81.3 us -> 38.3 us (0.47)
  the two profiles are of different devices: /device:TPU:8 before, /device:TPU:1 now
where the time goes in v1:
time: 38.3 us; the launch traced here: 38 us
  blocking collectives  19.3 us (50%)
  Pallas kernels  8.07 us (21%)
  local copies, waits for them, and re-layouts  5.4 us (14%)
  starting transfers between devices  4.6 us (12%)
  between operations  0.67 us (2%)
    all_to_all x1, blocking collectives, shards(): parts = lax.all_to_all(pay, 'dp', 0, 0, tiled=True)  19.3 us
    unnamed x14, local copies, waits for them, and re-layouts  5.4 us
    pallas_call x1, Pallas kernels, shards(): pl.pallas_call(finish, out_shape=(jax.ShapeDtypeStruct((ROWS, LANES), f32...  4.6 us
    pallas_call x1, Pallas kernels, shards(): pl.pallas_call(prepare, out_shape=(jax.ShapeDtypeStruct((N_DP, LANES), f3...  3.47 us
    ppermute x1, starting transfers between devices, shards(): from_next = lax.ppermute(send_next, 'dp', between)  2.94 us
    ppermute x1, starting transfers between devices, shards(): from_core = lax.ppermute(send_core, 'dp', pairs)  1.66 us
  transfers between devices with their start and end apart: 2, of which 0 were waited for; matrix products, arithmetic and copies ran while one was open for 0% of the time, Pallas kernels for 0%

profile of v1, /device:TPU:1, one launch (start us, length us, event | category | flops | bytes accessed | tf_op | source)
XLA Modules:
  0.0 38.0 jit_solution(17320885744523775084)
XLA Ops:
  0.6 0.0 copy-start.4
  0.6 0.0 copy-start.5
  0.7 0.7 %copy-done.4 = s32[129]{0:T(256)S(1)} copy-done((s32[129]{0:T(256)S(1)}, s32[129]{0:T(256)}, u32[]{:S(2)}) %copy-start.4) | copy-done | bytes 540
  1.3 0.0 copy-done.5
  1.3 0.0 copy-start
  1.3 1.0 %copy-done = f32[126976]{0:T(1024)S(1)} copy-done((f32[126976]{0:T(1024)S(1)}, f32[126976]{0:T(1024)}, u32[]{:S(2)}) %copy-start) | copy-done | bytes 507928
  2.4 0.0 copy-start.1
  2.4 1.0 %copy-done.1 = f32[126976]{0:T(1024)S(1)} copy-done((f32[126976]{0:T(1024)S(1)}, f32[126976]{0:T(1024)}, u32[]{:S(2)}) %copy-start.1) | copy-done | bytes 507928
  3.4 0.0 copy-start.2
  3.4 1.0 %copy-done.2 = f32[126976]{0:T(1024)S(1)} copy-done((f32[126976]{0:T(1024)S(1)}, f32[126976]{0:T(1024)}, u32[]{:S(2)}) %copy-start.2) | copy-done | bytes 507928
  4.4 0.0 copy-start.3
  4.4 0.9 %copy-done.3 = bf16[126976]{0:T(1024)(128)(2,1)S(1)} copy-done((bf16[126976]{0:T(1024)(128)(2,1)S(1)}, bf16[126976]{0:T(1024)(128)(2,1)}, u32[]{:S(2)}) %copy-start.3) | copy-done | bytes 253976
  5.4 3.5 %shard_map.94 = (f32[128,128]{1,0:T(8,128)S(1)}, f32[1032,128]{1,0:T(8,128)S(1)}, f32[1032,128]{1,0:T(8,128)S(1)}, f32[1032,128]{1,0:T(8,128)S(1)}, f32[1032,128...) custom-call(f32[992,128]{1,0:T(8,128)S(1)} %bitcast.11, f32[992,128]{1,0:T(8,128)S(1)} %bitcast.12, ...), custom_call_target="tpu_custom_call" | custom-call | tf_op jit(solution)/shard_map/pallas_call | solution.py:251
  8.8 1.7 %collective-permute-start = (f32[4,32,128]{2,1,0:T(8,128)S(1)}, f32[4,32,128]{2,1,0:T(8,128)S(1)}, u32[]{:S(2)}, u32[]{:S(2)}) collective-permute-start(f32[4,32,128]{2,1,0:T(8,128)S(1)} %get-tuple-element.18), channel_id=1, source_target_pairs={{0,1},{1,0},{2,3},{3,2},{4,5},{5,4},{6,7},{7,6},{8,9},{9,8},{10,11... | collective-permute-start | bytes 196616 | tf_op jit(solution)/shard_map/ppermute | solution.py:262
  10.5 2.9 %collective-permute-start.1 = (f32[4,32,128]{2,1,0:T(8,128)S(1)}, f32[4,32,128]{2,1,0:T(8,128)S(1)}, u32[]{:S(2)}, u32[]{:S(2)}) collective-permute-start(f32[4,32,128]{2,1,0:T(8,128)S(1)} %get-tuple-element.19), channel_id=1, source_target_pairs={{1,2},{3,4},{5,6},{7,8},{9,10},{11,12},{13,14},{15,16},{17,18},{19... | collective-permute-start | bytes 196616 | tf_op jit(solution)/shard_map/ppermute | solution.py:263
  13.5 19.3 %all_to_all.11 = f32[128,1,128]{2,1,0:T(1,128)S(1)} all-to-all(f32[128,1,128]{2,1,0:T(1,128)S(1)} %bitcast.16), channel_id=1, replica_groups=mesh['dp'=128] {'dp'}, dimensions={0} | all-to-all | bytes 131072 | tf_op jit(solution)/shard_map/all_to_all | solution.py:264
  32.7 0.0 collective-permute-done.from_core
  32.7 0.0 collective-permute-done.1.from_next
  32.7 0.0 copy-start.6
  32.7 0.7 %copy-done.6 = s32[129]{0:T(256)S(1)} copy-done((s32[129]{0:T(256)S(1)}, s32[129]{0:T(256)}, u32[]{:S(2)}) %copy-start.6) | copy-done | bytes 540
  33.4 4.6 %shard_map.95 = (f32[992,128]{1,0:T(8,128)}, f32[992,128]{1,0:T(8,128)}, f32[992,128]{1,0:T(8,128)}) custom-call(f32[128,128]{1,0:T(8,128)S(1)} %bitcast.14, f32[1032,128]{1,0:T(8,128)S(1)} %get-tuple-element.14.w_own, f32[1032,128]{1,0:T(8,128)S(1)} %get-tuple-element.15.m_own, f32[1032,128]{1,0:T(8,128)S(1)} %get-tuple-element.16.v_own, ...), custom_call_target="tpu_custom_call" | custom-call | tf_op jit(solution)/shard_map/pallas_call | solution.py:266
Async XLA Ops:
  0.6 0.7 %copy-start.4 = (s32[129]{0:T(256)S(1)}, s32[129]{0:T(256)}, u32[]{:S(2)}) copy-start(s32[129]{0:T(256)} %old.3) | copy-start | bytes 1552
  0.6 0.7 %copy-start.5 = (s32[64]{0:T(128)S(1)}, s32[64]{0:T(128)}, u32[]{:S(2)}) copy-start(s32[64]{0:T(128)} %seg.3) | copy-start | bytes 772
  1.3 1.0 %copy-start = (f32[126976]{0:T(1024)S(1)}, f32[126976]{0:T(1024)}, u32[]{:S(2)}) copy-start(f32[126976]{0:T(1024)} %param.7) | copy-start | bytes 1523716
  2.4 1.0 %copy-start.1 = (f32[126976]{0:T(1024)S(1)}, f32[126976]{0:T(1024)}, u32[]{:S(2)}) copy-start(f32[126976]{0:T(1024)} %param.8) | copy-start | bytes 1523716
  3.4 1.0 %copy-start.2 = (f32[126976]{0:T(1024)S(1)}, f32[126976]{0:T(1024)}, u32[]{:S(2)}) copy-start(f32[126976]{0:T(1024)} %param.9) | copy-start | bytes 1523716
  4.4 0.9 %copy-start.3 = (bf16[126976]{0:T(1024)(128)(2,1)S(1)}, bf16[126976]{0:T(1024)(128)(2,1)}, u32[]{:S(2)}) copy-start(bf16[126976]{0:T(1024)(128)(2,1)} %param.10) | copy-start | bytes 761860
  8.8 23.9 %collective-permute-start = (f32[4,32,128]{2,1,0:T(8,128)S(1)}, f32[4,32,128]{2,1,0:T(8,128)S(1)}, u32[]{:S(2)}, u32[]{:S(2)}) collective-permute-start(f32[4,32,128]{2,1,0:T(8,128)S(1)} %get-tuple-element.18), channel_id=1, source_target_pairs={{0,1},{1,0},{2,3},{3,2},{4,5},{5,4},{6,7},{7,6},{8,9},{9,8},{10,11... | collective-permute-start | bytes 196616 | tf_op jit(solution)/shard_map/ppermute | solution.py:262
  10.5 22.2 %collective-permute-start.1 = (f32[4,32,128]{2,1,0:T(8,128)S(1)}, f32[4,32,128]{2,1,0:T(8,128)S(1)}, u32[]{:S(2)}, u32[]{:S(2)}) collective-permute-start(f32[4,32,128]{2,1,0:T(8,128)S(1)} %get-tuple-element.19), channel_id=1, source_target_pairs={{1,2},{3,4},{5,6},{7,8},{9,10},{11,12},{13,14},{15,16},{17,18},{19... | collective-permute-start | bytes 196616 | tf_op jit(solution)/shard_map/ppermute | solution.py:263
  32.7 0.7 %copy-start.6 = (s32[129]{0:T(256)S(1)}, s32[129]{0:T(256)}, u32[]{:S(2)}) copy-start(s32[129]{0:T(256)} %new.1) | copy-start | bytes 1552

commit v2 on v1

--- a/solution.py
+++ b/solution.py
@@ -23,6 +23,8 @@
 
 BLOCK = 32
 BLOCK_ELEMS = BLOCK * LANES
+BLOCKS = ROWS // BLOCK
+PIECES = ((0, 8), (8, 16), (16, 24), (24, 31))
 
 
 def lanes_of(rows):
@@ -50,22 +52,34 @@
     return begin, end
 
 
-def prepare(w_hbm, m_hbm, v_hbm, g_hbm, old, seg, pay, w_own, m_own, v_own, u_own, send_core, send_next, m_in, v_in, g_in, sems):
-    copies = [
-        pltpu.make_async_copy(w_hbm, w_own.at[pl.ds(0, ROWS)], sems.at[0]),
-        pltpu.make_async_copy(m_hbm, m_in, sems.at[1]),
-        pltpu.make_async_copy(v_hbm, v_in, sems.at[2]),
-        pltpu.make_async_copy(g_hbm, g_in, sems.at[3]),
+def fold(x):
+    return x[0:8] + x[8:16] + x[16:24] + x[24:32]
+
+
+def prepare(w_hbm, m_hbm, v_hbm, g_hbm, old_hbm, seg_hbm, pay, w_own, m_own, v_own, u_own, send_core, send_next,
+            m_in, v_in, g_in, weight_sums, update_sums, old, seg, sems, scalar_sems):
+    scalar_copies = [
+        pltpu.make_async_copy(old_hbm, old, scalar_sems.at[0]),
+        pltpu.make_async_copy(seg_hbm, seg, scalar_sems.at[1]),
     ]
-    for copy in copies:
+    for copy in scalar_copies:
         copy.start()
+    pieces = []
+    for p, (begin, end) in enumerate(PIECES):
+        rows = pl.ds(begin * BLOCK, (end - begin) * BLOCK)
+        pieces.append([
+            pltpu.make_async_copy(source.at[rows], target.at[rows], sems.at[p, a])
+            for a, (source, target) in enumerate(((g_hbm, g_in), (v_hbm, v_in), (m_hbm, m_in), (w_hbm, w_own)))
+        ])
+        for copy in pieces[-1]:
+            copy.start()
     device = lax.axis_index("dp")
+    for copy in scalar_copies:
+        copy.wait()
     low = old[device]
     high = old[device + 1]
     count = high - low
     first, last = segment_range(seg, low, high)
-    for copy in copies:
-        copy.wait()
 
     def update(b, carry):
         rows = pl.ds(pl.multiple_of(b * BLOCK, BLOCK), BLOCK)
@@ -73,13 +87,19 @@
         weight = w_own[rows, :]
         moment = BETA_ONE * m_in[rows, :] + (1.0 - BETA_ONE) * grad
         second = BETA_TWO * v_in[rows, :] + (1.0 - BETA_TWO) * grad * grad
-        step = moment / CORR_ONE / (jnp.sqrt(second / CORR_TWO) + EPSILON) + DECAY * weight
+        step = moment * (1.0 / CORR_ONE) / (jnp.sqrt(second * (1.0 / CORR_TWO)) + EPSILON) + DECAY * weight
         m_own[rows, :] = moment
         v_own[rows, :] = second
         u_own[rows, :] = step
+        short = pl.ds(pl.multiple_of(b * 8, 8), 8)
+        weight_sums[short, :] = fold(weight * weight)
+        update_sums[short, :] = fold(step * step)
         return carry
 
-    lax.fori_loop(0, ROWS // BLOCK, update, 0)
+    for (begin, end), copies in zip(PIECES, pieces):
+        for copy in copies:
+            copy.wait()
+        lax.fori_loop(begin, end, update, 0, unroll=True)
 
     cut = count - MARGIN
     cut_row = cut // LANES
@@ -105,13 +125,12 @@
     element = index_of(BLOCK)
     lane = lanes_of(8)
 
-    def fold(x):
-        return x[0:8] + x[8:16] + x[16:24] + x[24:32]
-
     def segment(s, packed):
         begin, end = segment_span(seg, s, low, high)
-
-        def add(b, sums):
+        first_block = begin // BLOCK_ELEMS
+        last_block = (end - 1) // BLOCK_ELEMS
+
+        def edge(b, sums):
             weight_sum, update_sum = sums
             rows = pl.ds(pl.multiple_of(b * BLOCK, BLOCK), BLOCK)
             place = element + b * BLOCK_ELEMS
@@ -122,10 +141,15 @@
             update_sum = update_sum + fold(jnp.where(inside, step * step, 0.0))
             return weight_sum, update_sum
 
+        def whole(b, sums):
+            weight_sum, update_sum = sums
+            short = pl.ds(pl.multiple_of(b * 8, 8), 8)
+            return weight_sum + weight_sums[short, :], update_sum + update_sums[short, :]
+
         zero = jnp.zeros((8, LANES), jnp.float32)
-        weight_sum, update_sum = lax.fori_loop(
-            begin // BLOCK_ELEMS, (end + BLOCK_ELEMS - 1) // BLOCK_ELEMS, add, (zero, zero)
-        )
+        sums = edge(first_block, (zero, zero))
+        sums = lax.fori_loop(first_block + 1, last_block, whole, sums)
+        weight_sum, update_sum = lax.fori_loop(jnp.maximum(last_block, first_block + 1), last_block + 1, edge, sums)
         weight_sum = jnp.sum(weight_sum)
         update_sum = jnp.sum(update_sum)
         return packed + jnp.where(lane == s, weight_sum, 0.0) + jnp.where(lane == SEGS + s, update_sum, 0.0)
@@ -135,9 +159,20 @@
         pay[pl.ds(row, 8), :] = packed
 
 
-def finish(parts, w_own, m_own, v_own, u_own, from_core, from_next, old, new, seg, w_out, m_out, v_out,
-           w_new, m_new, v_new, u_new, heads, rims, sems):
+def finish(parts, w_own, m_own, v_own, u_own, from_core, from_next, old_hbm, new_hbm, seg_hbm, w_out, m_out, v_out,
+           w_new, m_new, v_new, u_new, heads, rims, old, new, seg, sems, scalar_sems):
+    scalar_copies = [
+        pltpu.make_async_copy(old_hbm, old, scalar_sems.at[0]),
+        pltpu.make_async_copy(new_hbm, new, scalar_sems.at[1]),
+        pltpu.make_async_copy(seg_hbm, seg, scalar_sems.at[2]),
+    ]
+    for copy in scalar_copies:
+        copy.start()
     device = lax.axis_index("dp")
+    sums = jnp.broadcast_to(jnp.sum(parts[...], axis=0, keepdims=True), (8, LANES))
+    ratio = jnp.sqrt(sums) / (jnp.sqrt(pltpu.roll(sums, SEGS, 1)) + EPSILON)
+    for copy in scalar_copies:
+        copy.wait()
     old_low = old[device]
     old_high = old[device + 1]
     low = new[device]
@@ -188,7 +223,7 @@
             news[a][rows, :] = moved(here, below, live)
         return carry
 
-    lax.fori_loop(1, ROWS // BLOCK, move, 0)
+    lax.fori_loop(1, BLOCKS, move, 0, unroll=6)
 
     cut = old_high - low
 
@@ -211,8 +246,6 @@
     m_copy.start()
     v_copy.start()
 
-    sums = jnp.broadcast_to(jnp.sum(parts[...], axis=0, keepdims=True), (8, LANES))
-    ratio = jnp.sqrt(sums) / (jnp.sqrt(pltpu.roll(sums, SEGS, 1)) + EPSILON)
     lane = lanes_of(8)
     first, last = segment_range(seg, low, high)
 
@@ -239,10 +272,16 @@
     w_copy.wait()
 
 
+def in_hbm(*arrays):
+    return [pltpu.with_memory_space_constraint(x, pltpu.HBM) for x in arrays]
+
+
 def shards(params, first_moment, second_moment, grads, old_bounds, new_bounds, seg_start):
-    any_space = pl.BlockSpec(memory_space=pl.ANY)
+    hbm = pl.BlockSpec(memory_space=pltpu.HBM)
     vmem = pl.BlockSpec(memory_space=pltpu.VMEM)
-    smem = pl.BlockSpec(memory_space=pltpu.SMEM)
+    bounds = pltpu.SMEM((N_DP + 1,), jnp.int32)
+    starts = pltpu.SMEM((SEGS,), jnp.int32)
+    block_sums = pltpu.VMEM((BLOCKS * 8, LANES), jnp.float32)
     f32 = jnp.float32
     own = jax.ShapeDtypeStruct((PAD_ROWS, LANES), f32)
     rim = jax.ShapeDtypeStruct((4, RIM, LANES), f32)
@@ -251,11 +290,12 @@
     pay, w_own, m_own, v_own, u_own, send_core, send_next = pl.pallas_call(
         prepare,
         out_shape=(jax.ShapeDtypeStruct((N_DP, LANES), f32), own, own, own, own, rim, rim),
-        in_specs=[any_space] * 4 + [smem] * 2,
+        in_specs=[hbm] * 6,
         out_specs=[vmem] * 7,
-        scratch_shapes=[state, state, pltpu.VMEM((ROWS, LANES), jnp.bfloat16), pltpu.SemaphoreType.DMA((4,))],
+        scratch_shapes=[state, state, pltpu.VMEM((ROWS, LANES), jnp.bfloat16), block_sums, block_sums, bounds, starts,
+                        pltpu.SemaphoreType.DMA((4, 4)), pltpu.SemaphoreType.DMA((2,))],
         compiler_params=pltpu.CompilerParams(vmem_limit_bytes=24 * 2**20),
-    )(*flat, old_bounds, seg_start)
+    )(*in_hbm(*flat, old_bounds, seg_start))
     pairs = [(i, i ^ 1) for i in range(N_DP)]
     between = [(i, i + 1) for i in range(1, N_DP - 1, 2)]
     between = between + [(j, i) for i, j in between]
@@ -266,12 +306,13 @@
     outs = pl.pallas_call(
         finish,
         out_shape=(jax.ShapeDtypeStruct((ROWS, LANES), f32),) * 3,
-        in_specs=[vmem] * 7 + [smem] * 3,
-        out_specs=[any_space] * 3,
+        in_specs=[vmem] * 7 + [hbm] * 3,
+        out_specs=[hbm] * 3,
         scratch_shapes=[padded] * 4
-        + [pltpu.VMEM((4, 104, LANES), f32), pltpu.VMEM((4, 48, LANES), f32), pltpu.SemaphoreType.DMA((3,))],
+        + [pltpu.VMEM((4, 104, LANES), f32), pltpu.VMEM((4, 48, LANES), f32), bounds, bounds, starts,
+           pltpu.SemaphoreType.DMA((3,)), pltpu.SemaphoreType.DMA((3,))],
         compiler_params=pltpu.CompilerParams(vmem_limit_bytes=24 * 2**20),
-    )(parts, w_own, m_own, v_own, u_own, from_core, from_next, old_bounds, new_bounds, seg_start)
+    )(parts, w_own, m_own, v_own, u_own, from_core, from_next, *in_hbm(old_bounds, new_bounds, seg_start))
     return tuple(x.reshape(-1) for x in outs)
 
 

time: 38.3 us -> 29.8 us (0.78)
  local copies, waits for them, and re-layouts: 5.4 us -> 0 us
  Pallas kernels: 8.07 us -> 5.2 us
    unnamed x14 -> x0, local copies, waits for them, and re-layouts: 5.4 us -> none
    pallas_call x1, Pallas kernels: 4.6 us -> 3.02 us  [shards(): pl.pallas_call(finish, out_shape=(jax.ShapeDtypeStruct((ROWS, LANES), f32...]
    pallas_call x1, Pallas kernels: 3.47 us -> 2.18 us  [shards(): pl.pallas_call(prepare, out_shape=(jax.ShapeDtypeStruct((N_DP, LANES), f3...]
where the time goes in v2:
time: 29.8 us; the launch traced here: 29.6 us
  blocking collectives  19.2 us (64%)
  Pallas kernels  5.2 us (17%)
  starting transfers between devices  4.6 us (15%)
  between operations  0.65 us (2%)
    all_to_all x1, blocking collectives, shards(): parts = lax.all_to_all(pay, 'dp', 0, 0, tiled=True)  19.2 us
    pallas_call x1, Pallas kernels, shards(): pl.pallas_call(finish, out_shape=(jax.ShapeDtypeStruct((ROWS, LANES), f32...  3.02 us
    ppermute x1, starting transfers between devices, shards(): from_next = lax.ppermute(send_next, 'dp', between)  2.95 us
    pallas_call x1, Pallas kernels, shards(): pl.pallas_call(prepare, out_shape=(jax.ShapeDtypeStruct((N_DP, LANES), f3...  2.18 us
    ppermute x1, starting transfers between devices, shards(): from_core = lax.ppermute(send_core, 'dp', pairs)  1.65 us
  transfers between devices with their start and end apart: 2, of which 0 were waited for; matrix products, arithmetic and copies ran while one was open for 0% of the time, Pallas kernels for 0%

profile of v2, /device:TPU:1, one launch (start us, length us, event | category | flops | bytes accessed | tf_op | source)
XLA Modules:
  0.0 29.6 jit_solution(12843229739264271888)
XLA Ops:
  0.6 2.2 %shard_map.94 = (f32[128,128]{1,0:T(8,128)S(1)}, f32[1032,128]{1,0:T(8,128)S(1)}, f32[1032,128]{1,0:T(8,128)S(1)}, f32[1032,128]{1,0:T(8,128)S(1)}, f32[1032,128...) custom-call(f32[992,128]{1,0:T(8,128)} %bitcast.13, f32[992,128]{1,0:T(8,128)} %bitcast.14, ...), custom_call_target="tpu_custom_call" | custom-call | tf_op jit(solution)/shard_map/pallas_call | solution.py:290
  2.8 1.6 %collective-permute-start = (f32[4,32,128]{2,1,0:T(8,128)S(1)}, f32[4,32,128]{2,1,0:T(8,128)S(1)}, u32[]{:S(2)}, u32[]{:S(2)}) collective-permute-start(f32[4,32,128]{2,1,0:T(8,128)S(1)} %get-tuple-element.18), channel_id=1, source_target_pairs={{0,1},{1,0},{2,3},{3,2},{4,5},{5,4},{6,7},{7,6},{8,9},{9,8},{10,11... | collective-permute-start | bytes 196616 | tf_op jit(solution)/shard_map/ppermute | solution.py:302
  4.5 3.0 %collective-permute-start.1 = (f32[4,32,128]{2,1,0:T(8,128)S(1)}, f32[4,32,128]{2,1,0:T(8,128)S(1)}, u32[]{:S(2)}, u32[]{:S(2)}) collective-permute-start(f32[4,32,128]{2,1,0:T(8,128)S(1)} %get-tuple-element.19), channel_id=1, source_target_pairs={{1,2},{3,4},{5,6},{7,8},{9,10},{11,12},{13,14},{15,16},{17,18},{19... | collective-permute-start | bytes 196616 | tf_op jit(solution)/shard_map/ppermute | solution.py:303
  7.4 19.2 %all_to_all.11 = f32[128,1,128]{2,1,0:T(1,128)S(1)} all-to-all(f32[128,1,128]{2,1,0:T(1,128)S(1)} %bitcast.12), channel_id=1, replica_groups=mesh['dp'=128] {'dp'}, dimensions={0} | all-to-all | bytes 131072 | tf_op jit(solution)/shard_map/all_to_all | solution.py:304
  26.6 0.0 collective-permute-done.from_core
  26.6 0.0 collective-permute-done.1.from_next
  26.6 3.0 %shard_map.95 = (f32[992,128]{1,0:T(8,128)}, f32[992,128]{1,0:T(8,128)}, f32[992,128]{1,0:T(8,128)}) custom-call(f32[128,128]{1,0:T(8,128)S(1)} %bitcast.11, f32[1032,128]{1,0:T(8,128)S(1)} %get-tuple-element.14.w_own, f32[1032,128]{1,0:T(8,128)S(1)} %get-tuple-element.15.m_own, f32[1032,128]{1,0:T(8,128)S(1)} %get-tuple-element.16.v_own, ...), custom_call_target="tpu_custom_call" | custom-call | tf_op jit(solution)/shard_map/pallas_call | solution.py:306
Async XLA Ops:
  2.8 23.8 %collective-permute-start = (f32[4,32,128]{2,1,0:T(8,128)S(1)}, f32[4,32,128]{2,1,0:T(8,128)S(1)}, u32[]{:S(2)}, u32[]{:S(2)}) collective-permute-start(f32[4,32,128]{2,1,0:T(8,128)S(1)} %get-tuple-element.18), channel_id=1, source_target_pairs={{0,1},{1,0},{2,3},{3,2},{4,5},{5,4},{6,7},{7,6},{8,9},{9,8},{10,11... | collective-permute-start | bytes 196616 | tf_op jit(solution)/shard_map/ppermute | solution.py:302
  4.5 22.1 %collective-permute-start.1 = (f32[4,32,128]{2,1,0:T(8,128)S(1)}, f32[4,32,128]{2,1,0:T(8,128)S(1)}, u32[]{:S(2)}, u32[]{:S(2)}) collective-permute-start(f32[4,32,128]{2,1,0:T(8,128)S(1)} %get-tuple-element.19), channel_id=1, source_target_pairs={{1,2},{3,4},{5,6},{7,8},{9,10},{11,12},{13,14},{15,16},{17,18},{19... | collective-permute-start | bytes 196616 | tf_op jit(solution)/shard_map/ppermute | solution.py:303

commit v3 on v2

v3 whole, which is shorter than its diff:
```python
import jax
import jax.numpy as jnp
from jax import lax
from jax.experimental import pallas as pl
from jax.experimental.pallas import tpu as pltpu
from jax.sharding import PartitionSpec as P

MARGIN = 4096
SEGS = 64
N_DP = 128
LANES = 128
ROWS = 992
RIM = MARGIN // LANES
PAD_ROWS = 1032
TAIL = 896
TAIL_ROWS = ROWS - TAIL

BETA_ONE = 0.9
BETA_TWO = 0.999
CORR_ONE = 1.0 - 0.9**10
CORR_TWO = 1.0 - 0.999**10
DECAY = 0.01
LEARN = 0.1
EPSILON = 1e-06

BLOCK = 32
BLOCK_ELEMS = BLOCK * LANES
BLOCKS = ROWS // BLOCK
PIECES = ((0, 8), (8, 16), (16, 24), (24, 31))


def lanes_of(rows):
    return lax.broadcasted_iota(jnp.int32, (rows, LANES), 1)


def index_of(rows):
    return lax.broadcasted_iota(jnp.int32, (rows, LANES), 0) * LANES + lanes_of(rows)


def segment_range(seg, low, high):
    first = jnp.int32(-1)
    last = jnp.int32(-1)
    for s in range(SEGS):
        start = seg[s]
        first = first + jnp.where(start <= low, 1, 0)
        last = last + jnp.where(start < high, 1, 0)
    return first, last


def segment_span(seg, s, low, high):
    begin = jnp.maximum(seg[s], low) - low
    following = jnp.where(s == SEGS - 1, high, seg[jnp.minimum(s + 1, SEGS - 1)])
    end = jnp.minimum(following, high) - low
    return begin, end


def is_early(device):
    return (device // 8 % 4 + device // 32 <= 1) & (device % 8 < 4)


def move_interior(owns, news, seg_map, seg, low, high, shift):
    shift_row = shift // LANES
    shift_lane = lax.rem(shift, LANES)
    back = lax.rem(LANES - shift_lane, LANES)
    keep = lanes_of(BLOCK) >= shift_lane

    def move(b, carry):
        source = b * BLOCK + shift_row - RIM
        rows = pl.ds(pl.multiple_of(b * BLOCK, BLOCK), BLOCK)
        for own, fresh in zip(owns, news):
            here = own[pl.ds(source, BLOCK), :]
            below = own[pl.ds(source + 1, BLOCK), :]
            fresh[rows, :] = pltpu.roll(jnp.where(keep, here, below), back, 1)
        return carry

    lax.fori_loop(1, BLOCKS, move, 0, unroll=6)
    first, last = segment_range(seg, low, high)
    element = index_of(BLOCK)

    def segment(s, carry):
        begin, end = segment_span(seg, s, low, high)
        first_block = begin // BLOCK_ELEMS
        last_block = jnp.where(s == last, BLOCKS - 1, (end - 1) // BLOCK_ELEMS)
        rows = pl.ds(pl.multiple_of(first_block * BLOCK, BLOCK), BLOCK)
        seg_map[rows, :] = jnp.where(element + first_block * BLOCK_ELEMS >= begin, s, seg_map[rows, :])

        def fill(b, inner):
            seg_map[pl.ds(pl.multiple_of(b * BLOCK, BLOCK), BLOCK), :] = jnp.full((BLOCK, LANES), s, jnp.int32)
            return inner

        lax.fori_loop(first_block + 1, last_block + 1, fill, 0)
        return carry

    lax.fori_loop(first, last + 1, segment, 0)


def fold(x):
    return x[0:8] + x[8:16] + x[16:24] + x[24:32]


def prepare(w_hbm, m_hbm, v_hbm, g_hbm, old_hbm, new_hbm, seg_hbm,
            pay, w_own, m_own, v_own, u_own, send_core, send_next, w_new, m_new, v_new, u_new, seg_map,
            m_in, v_in, g_in, weight_sums, update_sums, table, old, new, seg, sems, scalar_sems):
    scalar_copies = [
        pltpu.make_async_copy(old_hbm, old, scalar_sems.at[0]),
        pltpu.make_async_copy(seg_hbm, seg, scalar_sems.at[1]),
        pltpu.make_async_copy(new_hbm, new, scalar_sems.at[2]),
    ]
    for copy in scalar_copies:
        copy.start()
    pieces = []
    for p, (begin, end) in enumerate(PIECES):
        rows = pl.ds(begin * BLOCK, (end - begin) * BLOCK)
        pieces.append([
            pltpu.make_async_copy(source.at[rows], target.at[rows], sems.at[p, a])
            for a, (source, target) in enumerate(((g_hbm, g_in), (v_hbm, v_in), (m_hbm, m_in), (w_hbm, w_own)))
        ])
        for copy in pieces[-1]:
            copy.start()
    device = lax.axis_index("dp")
    table[...] = jnp.zeros((2 * SEGS, LANES), jnp.float32)
    for copy in scalar_copies:
        copy.wait()
    low = old[device]
    high = old[device + 1]
    count = high - low
    first, last = segment_range(seg, low, high)

    def update(b, carry):
        rows = pl.ds(pl.multiple_of(b * BLOCK, BLOCK), BLOCK)
        grad = g_in[rows, :].astype(jnp.float32)
        weight = w_own[rows, :]
        moment = BETA_ONE * m_in[rows, :] + (1.0 - BETA_ONE) * grad
        second = BETA_TWO * v_in[rows, :] + (1.0 - BETA_TWO) * grad * grad
        step = moment * (1.0 / CORR_ONE) / (jnp.sqrt(second * (1.0 / CORR_TWO)) + EPSILON) + DECAY * weight
        m_own[rows, :] = moment
        v_own[rows, :] = second
        u_own[rows, :] = step
        short = pl.ds(pl.multiple_of(b * 8, 8), 8)
        weight_sums[short, :] = fold(weight * weight)
        update_sums[short, :] = fold(step * step)
        return carry

    for (begin, end), copies in zip(PIECES, pieces):
        for copy in copies:
            copy.wait()
        lax.fori_loop(begin, end, update, 0, unroll=True)

    cut = count - MARGIN
    cut_row = cut // LANES
    cut_lane = lax.rem(cut, LANES)
    back = lax.rem(LANES - cut_lane, LANES)
    even = lax.rem(device, 2) == 0

    def write_rims(head, tail):
        for a, source in enumerate((w_own, m_own, v_own, u_own)):
            head[a] = source[pl.ds(0, RIM), :]
            here = source[pl.ds(cut_row, RIM), :]
            below = source[pl.ds(cut_row + 1, RIM), :]
            tail[a] = pltpu.roll(jnp.where(lanes_of(RIM) >= cut_lane, here, below), back, 1)

    @pl.when(even)
    def _():
        write_rims(send_next, send_core)

    @pl.when(jnp.logical_not(even))
    def _():
        write_rims(send_core, send_next)

    element = index_of(BLOCK)

    def segment(s, carry):
        begin, end = segment_span(seg, s, low, high)
        first_block = begin // BLOCK_ELEMS
        last_block = (end - 1) // BLOCK_ELEMS

        def edge(b, sums):
            weight_sum, update_sum = sums
            rows = pl.ds(pl.multiple_of(b * BLOCK, BLOCK), BLOCK)
            place = element + b * BLOCK_ELEMS
            inside = (place >= begin) & (place < end)
            weight = w_own[rows, :]
            step = u_own[rows, :]
            weight_sum = weight_sum + fold(jnp.where(inside, weight * weight, 0.0))
            update_sum = update_sum + fold(jnp.where(inside, step * step, 0.0))
            return weight_sum, update_sum

        def whole(b, sums):
            weight_sum, update_sum = sums
            short = pl.ds(pl.multiple_of(b * 8, 8), 8)
            return weight_sum + weight_sums[short, :], update_sum + update_sums[short, :]

        zero = jnp.zeros((8, LANES), jnp.float32)
        sums = edge(first_block, (zero, zero))
        sums = lax.fori_loop(first_block + 1, last_block, whole, sums)
        weight_sum, update_sum = lax.fori_loop(jnp.maximum(last_block, first_block + 1), last_block + 1, edge, sums)
        table[pl.ds(s, 1), :] = jnp.sum(weight_sum, axis=0, keepdims=True)
        table[pl.ds(SEGS + s, 1), :] = jnp.sum(update_sum, axis=0, keepdims=True)
        return carry

    lax.fori_loop(first, last + 1, segment, 0)
    packed = lax.dot_general(
        jnp.ones((8, LANES), jnp.float32), table[...], (((1,), (1,)), ((), ())),
        precision=lax.Precision.HIGHEST, preferred_element_type=jnp.float32,
    )
    for row in range(0, N_DP, 8):
        pay[pl.ds(row, 8), :] = packed

    @pl.when(is_early(device))
    def _():
        new_low = new[device]
        move_interior((w_own, m_own, v_own, u_own), (w_new, m_new, v_new, u_new), seg_map, seg,
                      new_low, new[device + 1], new_low - low + MARGIN)


def finish(parts, w_own, m_own, v_own, u_own, from_next, from_core, w_pre, m_pre, v_pre, u_pre, seg_pre,
           old_hbm, new_hbm, seg_hbm, w_out, m_out, v_out,
           w_late, m_late, v_late, u_late, seg_late, w_new, heads, tails, rims, old, new, seg, sems, scalar_sems):
    scalar_copies = [
        pltpu.make_async_copy(old_hbm, old, scalar_sems.at[0]),
        pltpu.make_async_copy(new_hbm, new, scalar_sems.at[1]),
        pltpu.make_async_copy(seg_hbm, seg, scalar_sems.at[2]),
    ]
    for copy in scalar_copies:
        copy.start()
    device = lax.axis_index("dp")
    early = is_early(device)
    owns = (w_own, m_own, v_own, u_own)
    outs = (w_out, m_out, v_out)
    body = pl.ds(RIM, TAIL - RIM)

    def wait_scalars():
        for copy in scalar_copies:
            copy.wait()

    def emit(news, seg_map, ready):
        body_copies = [pltpu.make_async_copy(news[a].at[body], outs[a].at[body], sems.at[a]) for a in (1, 2)]
        for copy in body_copies:
            copy.start()
        sums = jnp.broadcast_to(jnp.sum(parts[...], axis=0, keepdims=True), (8, LANES))
        rates = LEARN * jnp.sqrt(sums) / (jnp.sqrt(pltpu.roll(sums, SEGS, 1)) + EPSILON)

        def rate_of(labels):
            pieces = [jnp.take_along_axis(rates, labels[r:r + 8], axis=1) for r in range(0, labels.shape[0], 8)]
            return jnp.concatenate(pieces, axis=0)

        def apply(b, carry):
            rows = pl.ds(pl.multiple_of(b * BLOCK, BLOCK), BLOCK)
            w_new[rows, :] = news[0][rows, :] - rate_of(seg_map[rows, :]) * news[3][rows, :]
            return carry

        lax.fori_loop(1, TAIL // BLOCK, apply, 0, unroll=9)
        body_copies.append(pltpu.make_async_copy(w_new.at[body], w_out.at[body], sems.at[0]))
        body_copies[-1].start()
        if not ready:
            wait_scalars()

        low = new[device]
        count = new[device + 1] - low
        shift = low - old[device] + MARGIN
        shift_row = shift // LANES
        shift_lane = lax.rem(shift, LANES)
        back = lax.rem(LANES - shift_lane, LANES)
        even = lax.rem(device, 2) == 0

        def split_rims(left, right):
            for a in range(4):
                heads[a, pl.ds(0, RIM), :] = left[a]
                rims[a, pl.ds(8, RIM), :] = right[a]

        @pl.when(even)
        def _():
            split_rims(from_next, from_core)

        @pl.when(jnp.logical_not(even))
        def _():
            split_rims(from_core, from_next)

        keep = lanes_of(RIM) >= shift_lane
        tail_live = index_of(TAIL_ROWS) + TAIL * LANES < count
        for a in range(4):
            heads[a, pl.ds(RIM, 72), :] = owns[a][pl.ds(0, 72), :]
            here = heads[a, pl.ds(shift_row, RIM), :]
            below = heads[a, pl.ds(shift_row + 1, RIM), :]
            heads[a, pl.ds(104, RIM), :] = pltpu.roll(jnp.where(keep, here, below), back, 1)
            tails[a, pl.ds(0, TAIL_ROWS), :] = jnp.where(tail_live, news[a][pl.ds(TAIL, TAIL_ROWS), :], 0.0)
        cut = old[device + 1] - low

        @pl.when(cut < count)
        def _():
            cut_row = cut // LANES
            cut_lane = lax.rem(cut, LANES)
            place = index_of(40) + cut_row * LANES
            taken = (place >= cut) & (place < count)
            fits = lanes_of(40) < LANES - cut_lane
            rows = pl.ds(cut_row - TAIL, 40)
            for a in range(4):
                here = rims[a, pl.ds(8, 40), :]
                above = rims[a, pl.ds(7, 40), :]
                incoming = pltpu.roll(jnp.where(fits, here, above), cut_lane, 1)
                tails[a, rows, :] = jnp.where(taken, incoming, tails[a, rows, :])

        top = pl.ds(104, RIM)
        heads[0, top, :] = heads[0, top, :] - rate_of(seg_map[pl.ds(0, RIM), :]) * heads[3, top, :]
        bottom = pl.ds(0, TAIL_ROWS)
        tails[0, bottom, :] = tails[0, bottom, :] - rate_of(seg_map[pl.ds(TAIL, TAIL_ROWS), :]) * tails[3, bottom, :]
        edge_copies = []
        for a in range(3):
            edge_copies.append(pltpu.make_async_copy(heads.at[a, top], outs[a].at[pl.ds(0, RIM)], sems.at[3 + a]))
            edge_copies.append(
                pltpu.make_async_copy(tails.at[a, bottom], outs[a].at[pl.ds(TAIL, TAIL_ROWS)], sems.at[6 + a]))
        for copy in edge_copies:
            copy.start()
        for copy in body_copies + edge_copies:
            copy.wait()

    @pl.when(early)
    def _():
        emit((w_pre, m_pre, v_pre, u_pre), seg_pre, False)

    @pl.when(jnp.logical_not(early))
    def _():
        wait_scalars()
        news = (w_late, m_late, v_late, u_late)
        low = new[device]
        move_interior(owns, news, seg_late, seg, low, new[device + 1], low - old[device] + MARGIN)
        emit(news, seg_late, True)


def in_hbm(*arrays):
    return [pltpu.with_memory_space_constraint(x, pltpu.HBM) for x in arrays]


def shards(params, first_moment, second_moment, grads, old_bounds, new_bounds, seg_start):
    hbm = pl.BlockSpec(memory_space=pltpu.HBM)
    vmem = pl.BlockSpec(memory_space=pltpu.VMEM)
    bounds = pltpu.SMEM((N_DP + 1,), jnp.int32)
    starts = pltpu.SMEM((SEGS,), jnp.int32)
    block_sums = pltpu.VMEM((BLOCKS * 8, LANES), jnp.float32)
    f32 = jnp.float32
    own = jax.ShapeDtypeStruct((PAD_ROWS, LANES), f32)
    rim = jax.ShapeDtypeStruct((4, RIM, LANES), f32)
    state = pltpu.VMEM((ROWS, LANES), f32)
    flat = [x.reshape(ROWS, LANES) for x in (params, first_moment, second_moment, grads)]
    moved = jax.ShapeDtypeStruct((ROWS, LANES), f32)
    labels = jax.ShapeDtypeStruct((ROWS, LANES), jnp.int32)
    pay, w_own, m_own, v_own, u_own, send_core, send_next, *early = pl.pallas_call(
        prepare,
        out_shape=(jax.ShapeDtypeStruct((N_DP, LANES), f32), own, own, own, own, rim, rim,
                   moved, moved, moved, moved, labels),
        in_specs=[hbm] * 7,
        out_specs=[vmem] * 12,
        scratch_shapes=[state, state, pltpu.VMEM((ROWS, LANES), jnp.bfloat16), block_sums, block_sums,
                        pltpu.VMEM((2 * SEGS, LANES), f32), bounds, bounds, starts,
                        pltpu.SemaphoreType.DMA((4, 4)), pltpu.SemaphoreType.DMA((3,))],
        compiler_params=pltpu.CompilerParams(vmem_limit_bytes=24 * 2**20),
    )(*in_hbm(*flat, old_bounds, new_bounds, seg_start))
    pairs = [(i, i ^ 1) for i in range(N_DP)]
    between = [(i, (i + (1 if i % 2 else -1)) % N_DP) for i in range(N_DP)]
    from_next = lax.ppermute(send_next, "dp", between)
    from_core = lax.ppermute(send_core, "dp", pairs)
    parts = lax.all_to_all(pay, "dp", 0, 0, tiled=True)
    outs = pl.pallas_call(
        finish,
        out_shape=(jax.ShapeDtypeStruct((ROWS, LANES), f32),) * 3,
        in_specs=[vmem] * 12 + [hbm] * 3,
        out_specs=[hbm] * 3,
        scratch_shapes=[state] * 4 + [pltpu.VMEM((ROWS, LANES), jnp.int32), state]
        + [pltpu.VMEM((4, 136, LANES), f32), pltpu.VMEM((4, 136, LANES), f32), pltpu.VMEM((4, 48, LANES), f32),
           bounds, bounds, starts, pltpu.SemaphoreType.DMA((9,)), pltpu.SemaphoreType.DMA((3,))],
        compiler_params=pltpu.CompilerParams(vmem_limit_bytes=24 * 2**20),
    )(parts, w_own, m_own, v_own, u_own, from_next, from_core, *early, *in_hbm(old_bounds, new_bounds, seg_start))
    return tuple(x.reshape(-1) for x in outs)


def solution(mesh):
    return jax.shard_map(
        shards,
        mesh=mesh,
        in_specs=(P("dp"), P("dp"), P("dp"), P("dp"), P(), P(), P()),
        out_specs=(P("dp"), P("dp"), P("dp")),
        check_vma=False,
    )
```

time: 29.8 us -> 27.3 us (0.916)
  blocking collectives: 19.2 us -> 12.4 us
  starting transfers between devices: 4.6 us -> 8.52 us
    all_to_all x1, blocking collectives: 19.2 us -> 12.4 us  [shards(): parts = lax.all_to_all(pay, 'dp', 0, 0, tiled=True)]
    ppermute x1, starting transfers between devices: 1.65 us -> 5.85 us  [shards(): from_core = lax.ppermute(send_core, 'dp', pairs)]
    pallas_call x1, Pallas kernels: 2.18 us -> 3.53 us  [shards(): pl.pallas_call(prepare, out_shape=(jax.ShapeDtypeStruct((N_DP, LANES), f3...]
    pallas_call x1, Pallas kernels: 3.02 us -> 1.92 us  [shards(): pl.pallas_call(finish, out_shape=(jax.ShapeDtypeStruct((ROWS, LANES), f32...]
where the time goes in v3:
time: 27.3 us; the launch traced here: 27 us
  blocking collectives  12.4 us (45%)
  starting transfers between devices  8.52 us (31%)
  Pallas kernels  5.45 us (20%)
  between operations  0.64 us (2%)
    all_to_all x1, blocking collectives, shards(): parts = lax.all_to_all(pay, 'dp', 0, 0, tiled=True)  12.4 us
    ppermute x1, starting transfers between devices, shards(): from_core = lax.ppermute(send_core, 'dp', pairs)  5.85 us
    pallas_call x1, Pallas kernels, shards(): pl.pallas_call(prepare, out_shape=(jax.ShapeDtypeStruct((N_DP, LANES), f3...  3.53 us
    ppermute x1, starting transfers between devices, shards(): from_next = lax.ppermute(send_next, 'dp', between)  2.66 us
    pallas_call x1, Pallas kernels, shards(): pl.pallas_call(finish, out_shape=(jax.ShapeDtypeStruct((ROWS, LANES), f32...  1.92 us
  transfers between devices with their start and end apart: 2, of which 0 were waited for; matrix products, arithmetic and copies ran while one was open for 0% of the time, Pallas kernels for 0%

profile of v3, /device:TPU:1, one launch (start us, length us, event | category | flops | bytes accessed | tf_op | source)
XLA Modules:
  0.0 27.0 jit_solution(9375667879388992902)
XLA Ops:
  0.6 3.5 %shard_map.94 = (f32[128,128]{1,0:T(8,128)S(1)}, f32[1032,128]{1,0:T(8,128)S(1)}, f32[1032,128]{1,0:T(8,128)S(1)}, f32[1032,128]{1,0:T(8,128)S(1)}, f32[1032,128...) custom-call(f32[992,128]{1,0:T(8,128)} %bitcast.13, ...), custom_call_target="tpu_custom_call" | custom-call | tf_op jit(solution)/shard_map/pallas_call | solution.py:347
  4.2 2.7 %collective-permute-start = (f32[4,32,128]{2,1,0:T(8,128)S(1)}, f32[4,32,128]{2,1,0:T(8,128)S(1)}, u32[]{:S(2)}, u32[]{:S(2)}) collective-permute-start(f32[4,32,128]{2,1,0:T(8,128)S(1)} %get-tuple-element.23), channel_id=1, source_target_pairs={{0,127},{1,2},{2,1},{3,4},{4,3},{5,6},{6,5},{7,8},{8,7},{9,10},{10... | collective-permute-start | bytes 196616 | tf_op jit(solution)/shard_map/ppermute | solution.py:360
  6.8 5.9 %collective-permute-start.1 = (f32[4,32,128]{2,1,0:T(8,128)S(1)}, f32[4,32,128]{2,1,0:T(8,128)S(1)}, u32[]{:S(2)}, u32[]{:S(2)}) collective-permute-start(f32[4,32,128]{2,1,0:T(8,128)S(1)} %get-tuple-element.24), channel_id=1, source_target_pairs={{0,1},{1,0},{2,3},{3,2},{4,5},{5,4},{6,7},{7,6},{8,9},{9,8},{10,11... | collective-permute-start | bytes 196616 | tf_op jit(solution)/shard_map/ppermute | solution.py:361
  12.7 12.4 %all_to_all.11 = f32[128,1,128]{2,1,0:T(1,128)S(1)} all-to-all(f32[128,1,128]{2,1,0:T(1,128)S(1)} %bitcast.12), channel_id=1, replica_groups=mesh['dp'=128] {'dp'}, dimensions={0} | all-to-all | bytes 131072 | tf_op jit(solution)/shard_map/all_to_all | solution.py:362
  25.1 0.0 collective-permute-done.from_next
  25.1 0.0 collective-permute-done.1.from_core
  25.1 1.9 %shard_map.95 = (f32[992,128]{1,0:T(8,128)}, f32[992,128]{1,0:T(8,128)}, f32[992,128]{1,0:T(8,128)}) custom-call(f32[128,128]{1,0:T(8,128)S(1)} %bitcast.11, f32[1032,128]{1,0:T(8,128)S(1)} %get-tuple-element.19.w_own, f32[1032,128]{1,0:T(8,128)S(1)} %get-tuple-element.20.m_own, f32[1032,128]{1,0:T(8,128)S(1)} %get-tuple-element.21.v_own, ...), custom_call_target="tpu_custom_call" | custom-call | tf_op jit(solution)/shard_map/pallas_call | solution.py:363
Async XLA Ops:
  4.2 20.9 %collective-permute-start = (f32[4,32,128]{2,1,0:T(8,128)S(1)}, f32[4,32,128]{2,1,0:T(8,128)S(1)}, u32[]{:S(2)}, u32[]{:S(2)}) collective-permute-start(f32[4,32,128]{2,1,0:T(8,128)S(1)} %get-tuple-element.23), channel_id=1, source_target_pairs={{0,127},{1,2},{2,1},{3,4},{4,3},{5,6},{6,5},{7,8},{8,7},{9,10},{10... | collective-permute-start | bytes 196616 | tf_op jit(solution)/shard_map/ppermute | solution.py:360
  6.8 18.3 %collective-permute-start.1 = (f32[4,32,128]{2,1,0:T(8,128)S(1)}, f32[4,32,128]{2,1,0:T(8,128)S(1)}, u32[]{:S(2)}, u32[]{:S(2)}) collective-permute-start(f32[4,32,128]{2,1,0:T(8,128)S(1)} %get-tuple-element.24), channel_id=1, source_target_pairs={{0,1},{1,0},{2,3},{3,2},{4,5},{5,4},{6,7},{7,6},{8,9},{9,8},{10,11... | collective-permute-start | bytes 196616 | tf_op jit(solution)/shard_map/ppermute | solution.py:361

commit v4 on v3

--- a/solution.py
+++ b/solution.py
@@ -14,6 +14,7 @@
 PAD_ROWS = 1032
 TAIL = 896
 TAIL_ROWS = ROWS - TAIL
+BODY_PIECES = ((1, 14), (14, 22), (22, 28))
 
 BETA_ONE = 0.9
 BETA_TWO = 0.999
@@ -58,7 +59,7 @@
     return (device // 8 % 4 + device // 32 <= 1) & (device % 8 < 4)
 
 
-def move_interior(owns, news, seg_map, seg, low, high, shift):
+def move_interior(owns, news, shift):
     shift_row = shift // LANES
     shift_lane = lax.rem(shift, LANES)
     back = lax.rem(LANES - shift_lane, LANES)
@@ -73,7 +74,10 @@
             fresh[rows, :] = pltpu.roll(jnp.where(keep, here, below), back, 1)
         return carry
 
-    lax.fori_loop(1, BLOCKS, move, 0, unroll=6)
+    lax.fori_loop(1, BLOCKS, move, 0, unroll=True)
+
+
+def label_elements(seg_map, seg, low, high):
     first, last = segment_range(seg, low, high)
     element = index_of(BLOCK)
 
@@ -99,7 +103,7 @@
 
 
 def prepare(w_hbm, m_hbm, v_hbm, g_hbm, old_hbm, new_hbm, seg_hbm,
-            pay, w_own, m_own, v_own, u_own, send_core, send_next, w_new, m_new, v_new, u_new, seg_map,
+            pay, w_own, m_own, v_own, u_own, send_core, send_next, w_new, m_new, v_new, u_new, seg_map, info,
             m_in, v_in, g_in, weight_sums, update_sums, table, old, new, seg, sems, scalar_sems):
     scalar_copies = [
         pltpu.make_async_copy(old_hbm, old, scalar_sems.at[0]),
@@ -124,6 +128,12 @@
     low = old[device]
     high = old[device + 1]
     count = high - low
+    new_low = new[device]
+    new_high = new[device + 1]
+    row = lax.broadcasted_iota(jnp.int32, (8, LANES), 0)
+    facts = jnp.where(row == 0, new_low - low + MARGIN, new_low)
+    facts = jnp.where(row == 1, high - new_low, facts)
+    info[...] = jnp.where(row == 2, new_high - new_low, facts)
     first, last = segment_range(seg, low, high)
 
     def update(b, carry):
@@ -208,32 +218,25 @@
 
     @pl.when(is_early(device))
     def _():
-        new_low = new[device]
-        move_interior((w_own, m_own, v_own, u_own), (w_new, m_new, v_new, u_new), seg_map, seg,
-                      new_low, new[device + 1], new_low - low + MARGIN)
+        move_interior((w_own, m_own, v_own, u_own), (w_new, m_new, v_new, u_new), new_low - low + MARGIN)
+        label_elements(seg_map, seg, new_low, new_high)
 
 
 def finish(parts, w_own, m_own, v_own, u_own, from_next, from_core, w_pre, m_pre, v_pre, u_pre, seg_pre,
-           old_hbm, new_hbm, seg_hbm, w_out, m_out, v_out,
-           w_late, m_late, v_late, u_late, seg_late, w_new, heads, tails, rims, old, new, seg, sems, scalar_sems):
-    scalar_copies = [
-        pltpu.make_async_copy(old_hbm, old, scalar_sems.at[0]),
-        pltpu.make_async_copy(new_hbm, new, scalar_sems.at[1]),
-        pltpu.make_async_copy(seg_hbm, seg, scalar_sems.at[2]),
-    ]
-    for copy in scalar_copies:
-        copy.start()
+           info, seg_hbm, w_out, m_out, v_out,
+           w_late, m_late, v_late, u_late, seg_late, w_new, heads, tails, rims, seg, sems, seg_sem):
     device = lax.axis_index("dp")
+    facts = info[...]
+    shift = facts[0, 0]
+    cut = facts[1, 0]
+    count = facts[2, 0]
+    low = facts[3, 0]
     early = is_early(device)
     owns = (w_own, m_own, v_own, u_own)
     outs = (w_out, m_out, v_out)
     body = pl.ds(RIM, TAIL - RIM)
 
-    def wait_scalars():
-        for copy in scalar_copies:
-            copy.wait()
-
-    def emit(news, seg_map, ready):
+    def emit(news, seg_map):
         body_copies = [pltpu.make_async_copy(news[a].at[body], outs[a].at[body], sems.at[a]) for a in (1, 2)]
         for copy in body_copies:
             copy.start()
@@ -244,20 +247,6 @@
             pieces = [jnp.take_along_axis(rates, labels[r:r + 8], axis=1) for r in range(0, labels.shape[0], 8)]
             return jnp.concatenate(pieces, axis=0)
 
-        def apply(b, carry):
-            rows = pl.ds(pl.multiple_of(b * BLOCK, BLOCK), BLOCK)
-            w_new[rows, :] = news[0][rows, :] - rate_of(seg_map[rows, :]) * news[3][rows, :]
-            return carry
-
-        lax.fori_loop(1, TAIL // BLOCK, apply, 0, unroll=9)
-        body_copies.append(pltpu.make_async_copy(w_new.at[body], w_out.at[body], sems.at[0]))
-        body_copies[-1].start()
-        if not ready:
-            wait_scalars()
-
-        low = new[device]
-        count = new[device + 1] - low
-        shift = low - old[device] + MARGIN
         shift_row = shift // LANES
         shift_lane = lax.rem(shift, LANES)
         back = lax.rem(LANES - shift_lane, LANES)
@@ -284,7 +273,6 @@
             below = heads[a, pl.ds(shift_row + 1, RIM), :]
             heads[a, pl.ds(104, RIM), :] = pltpu.roll(jnp.where(keep, here, below), back, 1)
             tails[a, pl.ds(0, TAIL_ROWS), :] = jnp.where(tail_live, news[a][pl.ds(TAIL, TAIL_ROWS), :], 0.0)
-        cut = old[device + 1] - low
 
         @pl.when(cut < count)
         def _():
@@ -311,20 +299,33 @@
                 pltpu.make_async_copy(tails.at[a, bottom], outs[a].at[pl.ds(TAIL, TAIL_ROWS)], sems.at[6 + a]))
         for copy in edge_copies:
             copy.start()
+
+        def apply(b, carry):
+            rows = pl.ds(pl.multiple_of(b * BLOCK, BLOCK), BLOCK)
+            w_new[rows, :] = news[0][rows, :] - rate_of(seg_map[rows, :]) * news[3][rows, :]
+            return carry
+
+        for p, (begin, end) in enumerate(BODY_PIECES):
+            lax.fori_loop(begin, end, apply, 0, unroll=True)
+            rows = pl.ds(begin * BLOCK, (end - begin) * BLOCK)
+            body_copies.append(pltpu.make_async_copy(w_new.at[rows], w_out.at[rows], sems.at[9 + p]))
+            body_copies[-1].start()
         for copy in body_copies + edge_copies:
             copy.wait()
 
     @pl.when(early)
     def _():
-        emit((w_pre, m_pre, v_pre, u_pre), seg_pre, False)
+        emit((w_pre, m_pre, v_pre, u_pre), seg_pre)
 
     @pl.when(jnp.logical_not(early))
     def _():
-        wait_scalars()
+        copy = pltpu.make_async_copy(seg_hbm, seg, seg_sem)
+        copy.start()
         news = (w_late, m_late, v_late, u_late)
-        low = new[device]
-        move_interior(owns, news, seg_late, seg, low, new[device + 1], low - old[device] + MARGIN)
-        emit(news, seg_late, True)
+        move_interior(owns, news, shift)
+        copy.wait()
+        label_elements(seg_late, seg, low, low + count)
+        emit(news, seg_late)
 
 
 def in_hbm(*arrays):
@@ -347,9 +348,9 @@
     pay, w_own, m_own, v_own, u_own, send_core, send_next, *early = pl.pallas_call(
         prepare,
         out_shape=(jax.ShapeDtypeStruct((N_DP, LANES), f32), own, own, own, own, rim, rim,
-                   moved, moved, moved, moved, labels),
+                   moved, moved, moved, moved, labels, jax.ShapeDtypeStruct((8, LANES), jnp.int32)),
         in_specs=[hbm] * 7,
-        out_specs=[vmem] * 12,
+        out_specs=[vmem] * 13,
         scratch_shapes=[state, state, pltpu.VMEM((ROWS, LANES), jnp.bfloat16), block_sums, block_sums,
                         pltpu.VMEM((2 * SEGS, LANES), f32), bounds, bounds, starts,
                         pltpu.SemaphoreType.DMA((4, 4)), pltpu.SemaphoreType.DMA((3,))],
@@ -363,13 +364,13 @@
     outs = pl.pallas_call(
         finish,
         out_shape=(jax.ShapeDtypeStruct((ROWS, LANES), f32),) * 3,
-        in_specs=[vmem] * 12 + [hbm] * 3,
+        in_specs=[vmem] * 13 + [hbm],
         out_specs=[hbm] * 3,
         scratch_shapes=[state] * 4 + [pltpu.VMEM((ROWS, LANES), jnp.int32), state]
         + [pltpu.VMEM((4, 136, LANES), f32), pltpu.VMEM((4, 136, LANES), f32), pltpu.VMEM((4, 48, LANES), f32),
-           bounds, bounds, starts, pltpu.SemaphoreType.DMA((9,)), pltpu.SemaphoreType.DMA((3,))],
+           starts, pltpu.SemaphoreType.DMA((12,)), pltpu.SemaphoreType.DMA],
         compiler_params=pltpu.CompilerParams(vmem_limit_bytes=24 * 2**20),
-    )(parts, w_own, m_own, v_own, u_own, from_next, from_core, *early, *in_hbm(old_bounds, new_bounds, seg_start))
+    )(parts, w_own, m_own, v_own, u_own, from_next, from_core, *early, *in_hbm(seg_start))
     return tuple(x.reshape(-1) for x in outs)
 
 

time: 27.3 us -> 27 us (0.989)
  Pallas kernels: 5.45 us -> 4.83 us
  starting transfers between devices: 8.52 us -> 8.81 us
    ppermute x1, starting transfers between devices: 5.85 us -> 6.2 us  [shards(): from_core = lax.ppermute(send_core, 'dp', pairs)]
    pallas_call x1, Pallas kernels: 3.53 us -> 3.2 us  [shards(): pl.pallas_call(prepare, out_shape=(jax.ShapeDtypeStruct((N_DP, LANES), f3...]
    pallas_call x1, Pallas kernels: 1.92 us -> 1.63 us  [shards(): pl.pallas_call(finish, out_shape=(jax.ShapeDtypeStruct((ROWS, LANES), f32...]
where the time goes in v4:
time: 27 us; the launch traced here: 26.8 us
  blocking collectives  12.5 us (46%)
  starting transfers between devices  8.81 us (33%)
  Pallas kernels  4.83 us (18%)
  between operations  0.64 us (2%)
    all_to_all x1, blocking collectives, shards(): parts = lax.all_to_all(pay, 'dp', 0, 0, tiled=True)  12.5 us
    ppermute x1, starting transfers between devices, shards(): from_core = lax.ppermute(send_core, 'dp', pairs)  6.2 us
    pallas_call x1, Pallas kernels, shards(): pl.pallas_call(prepare, out_shape=(jax.ShapeDtypeStruct((N_DP, LANES), f3...  3.2 us
    ppermute x1, starting transfers between devices, shards(): from_next = lax.ppermute(send_next, 'dp', between)  2.61 us
    pallas_call x1, Pallas kernels, shards(): pl.pallas_call(finish, out_shape=(jax.ShapeDtypeStruct((ROWS, LANES), f32...  1.63 us
  transfers between devices with their start and end apart: 2, of which 0 were waited for; matrix products, arithmetic and copies ran while one was open for 0% of the time, Pallas kernels for 0%

profile of v4, /device:TPU:1, one launch (start us, length us, event | category | flops | bytes accessed | tf_op | source)
XLA Modules:
  0.0 26.8 jit_solution(12028381364901487744)
XLA Ops:
  0.6 3.2 %shard_map.94 = (f32[128,128]{1,0:T(8,128)S(1)}, f32[1032,128]{1,0:T(8,128)S(1)}, f32[1032,128]{1,0:T(8,128)S(1)}, f32[1032,128]{1,0:T(8,128)S(1)}, f32[1032,128...) custom-call(f32[992,128]{1,0:T(8,128)} %bitcast.13, ...), custom_call_target="tpu_custom_call" | custom-call | tf_op jit(solution)/shard_map/pallas_call | solution.py:348
  3.8 2.6 %collective-permute-start = (f32[4,32,128]{2,1,0:T(8,128)S(1)}, f32[4,32,128]{2,1,0:T(8,128)S(1)}, u32[]{:S(2)}, u32[]{:S(2)}) collective-permute-start(f32[4,32,128]{2,1,0:T(8,128)S(1)} %get-tuple-element.24), channel_id=1, source_target_pairs={{0,127},{1,2},{2,1},{3,4},{4,3},{5,6},{6,5},{7,8},{8,7},{9,10},{10... | collective-permute-start | bytes 196616 | tf_op jit(solution)/shard_map/ppermute | solution.py:361
  6.5 6.2 %collective-permute-start.1 = (f32[4,32,128]{2,1,0:T(8,128)S(1)}, f32[4,32,128]{2,1,0:T(8,128)S(1)}, u32[]{:S(2)}, u32[]{:S(2)}) collective-permute-start(f32[4,32,128]{2,1,0:T(8,128)S(1)} %get-tuple-element.25), channel_id=1, source_target_pairs={{0,1},{1,0},{2,3},{3,2},{4,5},{5,4},{6,7},{7,6},{8,9},{9,8},{10,11... | collective-permute-start | bytes 196616 | tf_op jit(solution)/shard_map/ppermute | solution.py:362
  12.7 12.5 %all_to_all.11 = f32[128,1,128]{2,1,0:T(1,128)S(1)} all-to-all(f32[128,1,128]{2,1,0:T(1,128)S(1)} %bitcast.12), channel_id=1, replica_groups=mesh['dp'=128] {'dp'}, dimensions={0} | all-to-all | bytes 131072 | tf_op jit(solution)/shard_map/all_to_all | solution.py:363
  25.2 0.0 collective-permute-done.from_next
  25.2 0.0 collective-permute-done.1.from_core
  25.2 1.6 %shard_map.95 = (f32[992,128]{1,0:T(8,128)}, f32[992,128]{1,0:T(8,128)}, f32[992,128]{1,0:T(8,128)}) custom-call(f32[128,128]{1,0:T(8,128)S(1)} %bitcast.11, f32[1032,128]{1,0:T(8,128)S(1)} %get-tuple-element.20.w_own, f32[1032,128]{1,0:T(8,128)S(1)} %get-tuple-element.21.m_own, f32[1032,128]{1,0:T(8,128)S(1)} %get-tuple-element.22.v_own, ...), custom_call_target="tpu_custom_call" | custom-call | tf_op jit(solution)/shard_map/pallas_call | solution.py:364
Async XLA Ops:
  3.8 21.3 %collective-permute-start = (f32[4,32,128]{2,1,0:T(8,128)S(1)}, f32[4,32,128]{2,1,0:T(8,128)S(1)}, u32[]{:S(2)}, u32[]{:S(2)}) collective-permute-start(f32[4,32,128]{2,1,0:T(8,128)S(1)} %get-tuple-element.24), channel_id=1, source_target_pairs={{0,127},{1,2},{2,1},{3,4},{4,3},{5,6},{6,5},{7,8},{8,7},{9,10},{10... | collective-permute-start | bytes 196616 | tf_op jit(solution)/shard_map/ppermute | solution.py:361
  6.5 18.7 %collective-permute-start.1 = (f32[4,32,128]{2,1,0:T(8,128)S(1)}, f32[4,32,128]{2,1,0:T(8,128)S(1)}, u32[]{:S(2)}, u32[]{:S(2)}) collective-permute-start(f32[4,32,128]{2,1,0:T(8,128)S(1)} %get-tuple-element.25), channel_id=1, source_target_pairs={{0,1},{1,0},{2,3},{3,2},{4,5},{5,4},{6,7},{7,6},{8,9},{9,8},{10,11... | collective-permute-start | bytes 196616 | tf_op jit(solution)/shard_map/ppermute | solution.py:362

commit v5 on v4

--- a/solution.py
+++ b/solution.py
@@ -39,12 +39,11 @@
 
 
 def segment_range(seg, low, high):
-    first = jnp.int32(-1)
-    last = jnp.int32(-1)
-    for s in range(SEGS):
-        start = seg[s]
-        first = first + jnp.where(start <= low, 1, 0)
-        last = last + jnp.where(start < high, 1, 0)
+    first = jnp.int32(0)
+    last = jnp.int32(0)
+    for step in (32, 16, 8, 4, 2, 1):
+        first = first + jnp.where(seg[first + step] <= low, step, 0)
+        last = last + jnp.where(seg[last + step] < high, step, 0)
     return first, last
 
 
@@ -122,7 +121,7 @@
         for copy in pieces[-1]:
             copy.start()
     device = lax.axis_index("dp")
-    table[...] = jnp.zeros((2 * SEGS, LANES), jnp.float32)
+    even = lax.rem(device, 2) == 0
     for copy in scalar_copies:
         copy.wait()
     low = old[device]
@@ -160,26 +159,19 @@
     cut_row = cut // LANES
     cut_lane = lax.rem(cut, LANES)
     back = lax.rem(LANES - cut_lane, LANES)
-    even = lax.rem(device, 2) == 0
-
-    def write_rims(head, tail):
-        for a, source in enumerate((w_own, m_own, v_own, u_own)):
-            head[a] = source[pl.ds(0, RIM), :]
-            here = source[pl.ds(cut_row, RIM), :]
-            below = source[pl.ds(cut_row + 1, RIM), :]
-            tail[a] = pltpu.roll(jnp.where(lanes_of(RIM) >= cut_lane, here, below), back, 1)
-
-    @pl.when(even)
-    def _():
-        write_rims(send_next, send_core)
-
-    @pl.when(jnp.logical_not(even))
-    def _():
-        write_rims(send_core, send_next)
+    for a, source in enumerate((w_own, m_own, v_own, u_own)):
+        here = source[pl.ds(cut_row, RIM), :]
+        below = source[pl.ds(cut_row + 1, RIM), :]
+        tail = pltpu.roll(jnp.where(lanes_of(RIM) >= cut_lane, here, below), back, 1)
+        head = source[pl.ds(0, RIM), :]
+        send_next[a] = jnp.where(even, head, tail)
+        send_core[a] = jnp.where(even, tail, head)
 
     element = index_of(BLOCK)
 
-    def segment(s, carry):
+    lane = lanes_of(8)
+
+    def segment(s, packed):
         begin, end = segment_span(seg, s, low, high)
         first_block = begin // BLOCK_ELEMS
         last_block = (end - 1) // BLOCK_ELEMS
@@ -195,24 +187,25 @@
             update_sum = update_sum + fold(jnp.where(inside, step * step, 0.0))
             return weight_sum, update_sum
 
-        def whole(b, sums):
+        def whole(group, sums):
             weight_sum, update_sum = sums
-            short = pl.ds(pl.multiple_of(b * 8, 8), 8)
-            return weight_sum + weight_sums[short, :], update_sum + update_sums[short, :]
+            for b in range(8):
+                block = group * 8 + b
+                inner = (block > first_block) & (block < last_block)
+                short = pl.ds(pl.multiple_of(group * 64 + b * 8, 8), 8)
+                weight_sum = weight_sum + jnp.where(inner, weight_sums[short, :], 0.0)
+                update_sum = update_sum + jnp.where(inner, update_sums[short, :], 0.0)
+            return weight_sum, update_sum
 
         zero = jnp.zeros((8, LANES), jnp.float32)
         sums = edge(first_block, (zero, zero))
-        sums = lax.fori_loop(first_block + 1, last_block, whole, sums)
+        sums = lax.fori_loop((first_block + 1) // 8, (last_block + 7) // 8, whole, sums)
         weight_sum, update_sum = lax.fori_loop(jnp.maximum(last_block, first_block + 1), last_block + 1, edge, sums)
-        table[pl.ds(s, 1), :] = jnp.sum(weight_sum, axis=0, keepdims=True)
-        table[pl.ds(SEGS + s, 1), :] = jnp.sum(update_sum, axis=0, keepdims=True)
-        return carry
-
-    lax.fori_loop(first, last + 1, segment, 0)
-    packed = lax.dot_general(
-        jnp.ones((8, LANES), jnp.float32), table[...], (((1,), (1,)), ((), ())),
-        precision=lax.Precision.HIGHEST, preferred_element_type=jnp.float32,
-    )
+        weight_sum = jnp.sum(jnp.sum(weight_sum, axis=0, keepdims=True), axis=1, keepdims=True)
+        update_sum = jnp.sum(jnp.sum(update_sum, axis=0, keepdims=True), axis=1, keepdims=True)
+        return packed + jnp.where(lane == s, weight_sum, 0.0) + jnp.where(lane == SEGS + s, update_sum, 0.0)
+
+    packed = lax.fori_loop(first, last + 1, segment, jnp.zeros((8, LANES), jnp.float32))
     for row in range(0, N_DP, 8):
         pay[pl.ds(row, 8), :] = packed
 
@@ -247,23 +240,24 @@
             pieces = [jnp.take_along_axis(rates, labels[r:r + 8], axis=1) for r in range(0, labels.shape[0], 8)]
             return jnp.concatenate(pieces, axis=0)
 
+        def apply(b, carry):
+            rows = pl.ds(pl.multiple_of(b * BLOCK, BLOCK), BLOCK)
+            w_new[rows, :] = news[0][rows, :] - rate_of(seg_map[rows, :]) * news[3][rows, :]
+            return carry
+
+        for p, (begin, end) in enumerate(BODY_PIECES):
+            lax.fori_loop(begin, end, apply, 0, unroll=True)
+            rows = pl.ds(begin * BLOCK, (end - begin) * BLOCK)
+            body_copies.append(pltpu.make_async_copy(w_new.at[rows], w_out.at[rows], sems.at[9 + p]))
+            body_copies[-1].start()
         shift_row = shift // LANES
         shift_lane = lax.rem(shift, LANES)
         back = lax.rem(LANES - shift_lane, LANES)
         even = lax.rem(device, 2) == 0
 
-        def split_rims(left, right):
-            for a in range(4):
-                heads[a, pl.ds(0, RIM), :] = left[a]
-                rims[a, pl.ds(8, RIM), :] = right[a]
-
-        @pl.when(even)
-        def _():
-            split_rims(from_next, from_core)
-
-        @pl.when(jnp.logical_not(even))
-        def _():
-            split_rims(from_core, from_next)
+        for a in range(4):
+            heads[a, pl.ds(0, RIM), :] = jnp.where(even, from_next[a], from_core[a])
+            rims[a, pl.ds(8, RIM), :] = jnp.where(even, from_core[a], from_next[a])
 
         keep = lanes_of(RIM) >= shift_lane
         tail_live = index_of(TAIL_ROWS) + TAIL * LANES < count
@@ -274,19 +268,17 @@
             heads[a, pl.ds(104, RIM), :] = pltpu.roll(jnp.where(keep, here, below), back, 1)
             tails[a, pl.ds(0, TAIL_ROWS), :] = jnp.where(tail_live, news[a][pl.ds(TAIL, TAIL_ROWS), :], 0.0)
 
-        @pl.when(cut < count)
-        def _():
-            cut_row = cut // LANES
-            cut_lane = lax.rem(cut, LANES)
-            place = index_of(40) + cut_row * LANES
-            taken = (place >= cut) & (place < count)
-            fits = lanes_of(40) < LANES - cut_lane
-            rows = pl.ds(cut_row - TAIL, 40)
-            for a in range(4):
-                here = rims[a, pl.ds(8, 40), :]
-                above = rims[a, pl.ds(7, 40), :]
-                incoming = pltpu.roll(jnp.where(fits, here, above), cut_lane, 1)
-                tails[a, rows, :] = jnp.where(taken, incoming, tails[a, rows, :])
+        cut_row = jnp.minimum(cut // LANES - TAIL, TAIL_ROWS)
+        cut_lane = lax.rem(cut, LANES)
+        place = index_of(40) + (cut_row + TAIL) * LANES
+        taken = (place >= cut) & (place < count)
+        fits = lanes_of(40) < LANES - cut_lane
+        rows = pl.ds(cut_row, 40)
+        for a in range(4):
+            here = rims[a, pl.ds(8, 40), :]
+            above = rims[a, pl.ds(7, 40), :]
+            incoming = pltpu.roll(jnp.where(fits, here, above), cut_lane, 1)
+            tails[a, rows, :] = jnp.where(taken, incoming, tails[a, rows, :])
 
         top = pl.ds(104, RIM)
         heads[0, top, :] = heads[0, top, :] - rate_of(seg_map[pl.ds(0, RIM), :]) * heads[3, top, :]
@@ -300,16 +292,6 @@
         for copy in edge_copies:
             copy.start()
 
-        def apply(b, carry):
-            rows = pl.ds(pl.multiple_of(b * BLOCK, BLOCK), BLOCK)
-            w_new[rows, :] = news[0][rows, :] - rate_of(seg_map[rows, :]) * news[3][rows, :]
-            return carry
-
-        for p, (begin, end) in enumerate(BODY_PIECES):
-            lax.fori_loop(begin, end, apply, 0, unroll=True)
-            rows = pl.ds(begin * BLOCK, (end - begin) * BLOCK)
-            body_copies.append(pltpu.make_async_copy(w_new.at[rows], w_out.at[rows], sems.at[9 + p]))
-            body_copies[-1].start()
         for copy in body_copies + edge_copies:
             copy.wait()
 
@@ -337,7 +319,7 @@
     vmem = pl.BlockSpec(memory_space=pltpu.VMEM)
     bounds = pltpu.SMEM((N_DP + 1,), jnp.int32)
     starts = pltpu.SMEM((SEGS,), jnp.int32)
-    block_sums = pltpu.VMEM((BLOCKS * 8, LANES), jnp.float32)
+    block_sums = pltpu.VMEM((32 * 8, LANES), jnp.float32)
     f32 = jnp.float32
     own = jax.ShapeDtypeStruct((PAD_ROWS, LANES), f32)
     rim = jax.ShapeDtypeStruct((4, RIM, LANES), f32)

time: 27 us -> 26.7 us (0.989)
  Pallas kernels: 4.83 us -> 4.47 us
where the time goes in v5:
time: 26.7 us; the launch traced here: 26.5 us
  blocking collectives  12.6 us (47%)
  starting transfers between devices  8.75 us (33%)
  Pallas kernels  4.47 us (17%)
  between operations  0.64 us (2%)
    all_to_all x1, blocking collectives, shards(): parts = lax.all_to_all(pay, 'dp', 0, 0, tiled=True)  12.6 us
    ppermute x1, starting transfers between devices, shards(): from_core = lax.ppermute(send_core, 'dp', pairs)  6.21 us
    pallas_call x1, Pallas kernels, shards(): pl.pallas_call(prepare, out_shape=(jax.ShapeDtypeStruct((N_DP, LANES), f3...  3.06 us
    ppermute x1, starting transfers between devices, shards(): from_next = lax.ppermute(send_next, 'dp', between)  2.54 us
    pallas_call x1, Pallas kernels, shards(): pl.pallas_call(finish, out_shape=(jax.ShapeDtypeStruct((ROWS, LANES), f32...  1.41 us
  transfers between devices with their start and end apart: 2, of which 0 were waited for; matrix products, arithmetic and copies ran while one was open for 0% of the time, Pallas kernels for 0%

profile of v5, /device:TPU:1, one launch (start us, length us, event | category | flops | bytes accessed | tf_op | source)
XLA Modules:
  0.0 26.5 jit_solution(12086922865856451892)
XLA Ops:
  0.6 3.1 %shard_map.94 = (f32[128,128]{1,0:T(8,128)S(1)}, f32[1032,128]{1,0:T(8,128)S(1)}, f32[1032,128]{1,0:T(8,128)S(1)}, f32[1032,128]{1,0:T(8,128)S(1)}, f32[1032,128...) custom-call(f32[992,128]{1,0:T(8,128)} %bitcast.13, ...), custom_call_target="tpu_custom_call" | custom-call | tf_op jit(solution)/shard_map/pallas_call | solution.py:330
  3.7 2.5 %collective-permute-start = (f32[4,32,128]{2,1,0:T(8,128)S(1)}, f32[4,32,128]{2,1,0:T(8,128)S(1)}, u32[]{:S(2)}, u32[]{:S(2)}) collective-permute-start(f32[4,32,128]{2,1,0:T(8,128)S(1)} %get-tuple-element.24), channel_id=1, source_target_pairs={{0,127},{1,2},{2,1},{3,4},{4,3},{5,6},{6,5},{7,8},{8,7},{9,10},{10... | collective-permute-start | bytes 196616 | tf_op jit(solution)/shard_map/ppermute | solution.py:343
  6.2 6.2 %collective-permute-start.1 = (f32[4,32,128]{2,1,0:T(8,128)S(1)}, f32[4,32,128]{2,1,0:T(8,128)S(1)}, u32[]{:S(2)}, u32[]{:S(2)}) collective-permute-start(f32[4,32,128]{2,1,0:T(8,128)S(1)} %get-tuple-element.25), channel_id=1, source_target_pairs={{0,1},{1,0},{2,3},{3,2},{4,5},{5,4},{6,7},{7,6},{8,9},{9,8},{10,11... | collective-permute-start | bytes 196616 | tf_op jit(solution)/shard_map/ppermute | solution.py:344
  12.5 12.6 %all_to_all.11 = f32[128,1,128]{2,1,0:T(1,128)S(1)} all-to-all(f32[128,1,128]{2,1,0:T(1,128)S(1)} %bitcast.12), channel_id=1, replica_groups=mesh['dp'=128] {'dp'}, dimensions={0} | all-to-all | bytes 131072 | tf_op jit(solution)/shard_map/all_to_all | solution.py:345
  25.1 0.0 collective-permute-done.from_next
  25.1 0.0 collective-permute-done.1.from_core
  25.1 1.4 %shard_map.95 = (f32[992,128]{1,0:T(8,128)}, f32[992,128]{1,0:T(8,128)}, f32[992,128]{1,0:T(8,128)}) custom-call(f32[128,128]{1,0:T(8,128)S(1)} %bitcast.11, f32[1032,128]{1,0:T(8,128)S(1)} %get-tuple-element.20.w_own, f32[1032,128]{1,0:T(8,128)S(1)} %get-tuple-element.21.m_own, f32[1032,128]{1,0:T(8,128)S(1)} %get-tuple-element.22.v_own, ...), custom_call_target="tpu_custom_call" | custom-call | tf_op jit(solution)/shard_map/pallas_call | solution.py:346
Async XLA Ops:
  3.7 21.4 %collective-permute-start = (f32[4,32,128]{2,1,0:T(8,128)S(1)}, f32[4,32,128]{2,1,0:T(8,128)S(1)}, u32[]{:S(2)}, u32[]{:S(2)}) collective-permute-start(f32[4,32,128]{2,1,0:T(8,128)S(1)} %get-tuple-element.24), channel_id=1, source_target_pairs={{0,127},{1,2},{2,1},{3,4},{4,3},{5,6},{6,5},{7,8},{8,7},{9,10},{10... | collective-permute-start | bytes 196616 | tf_op jit(solution)/shard_map/ppermute | solution.py:343
  6.2 18.8 %collective-permute-start.1 = (f32[4,32,128]{2,1,0:T(8,128)S(1)}, f32[4,32,128]{2,1,0:T(8,128)S(1)}, u32[]{:S(2)}, u32[]{:S(2)}) collective-permute-start(f32[4,32,128]{2,1,0:T(8,128)S(1)} %get-tuple-element.25), channel_id=1, source_target_pairs={{0,1},{1,0},{2,3},{3,2},{4,5},{5,4},{6,7},{7,6},{8,9},{9,8},{10,11... | collective-permute-start | bytes 196616 | tf_op jit(solution)/shard_map/ppermute | solution.py:344

commit v6 on v5

--- a/solution.py
+++ b/solution.py
@@ -27,6 +27,7 @@
 BLOCK = 32
 BLOCK_ELEMS = BLOCK * LANES
 BLOCKS = ROWS // BLOCK
+LIVE = 29
 PIECES = ((0, 8), (8, 16), (16, 24), (24, 31))
 
 
@@ -103,7 +104,7 @@
 
 def prepare(w_hbm, m_hbm, v_hbm, g_hbm, old_hbm, new_hbm, seg_hbm,
             pay, w_own, m_own, v_own, u_own, send_core, send_next, w_new, m_new, v_new, u_new, seg_map, info,
-            m_in, v_in, g_in, weight_sums, update_sums, table, old, new, seg, sems, scalar_sems):
+            m_in, v_in, g_in, weight_sums, update_sums, old, new, seg, sems, scalar_sems):
     scalar_copies = [
         pltpu.make_async_copy(old_hbm, old, scalar_sems.at[0]),
         pltpu.make_async_copy(seg_hbm, seg, scalar_sems.at[1]),
@@ -146,14 +147,19 @@
         v_own[rows, :] = second
         u_own[rows, :] = step
         short = pl.ds(pl.multiple_of(b * 8, 8), 8)
-        weight_sums[short, :] = fold(weight * weight)
-        update_sums[short, :] = fold(step * step)
-        return carry
-
+        weight_sum = fold(weight * weight)
+        update_sum = fold(step * step)
+        weight_sums[short, :] = weight_sum
+        update_sums[short, :] = update_sum
+        return carry[0] + weight_sum, carry[1] + update_sum
+
+    zero = jnp.zeros((8, LANES), jnp.float32)
+    live_sums = (zero, zero)
     for (begin, end), copies in zip(PIECES, pieces):
         for copy in copies:
             copy.wait()
-        lax.fori_loop(begin, end, update, 0, unroll=True)
+        live_sums = lax.fori_loop(begin, min(end, LIVE), update, live_sums, unroll=True)
+        lax.fori_loop(min(end, LIVE), end, update, (zero, zero), unroll=True)
 
     cut = count - MARGIN
     cut_row = cut // LANES
@@ -171,21 +177,29 @@
 
     lane = lanes_of(8)
 
+    def masked(b, sums, begin, end):
+        weight_sum, update_sum = sums
+        rows = pl.ds(pl.multiple_of(b * BLOCK, BLOCK), BLOCK)
+        place = element + b * BLOCK_ELEMS
+        inside = (place >= begin) & (place < end)
+        weight = w_own[rows, :]
+        step = u_own[rows, :]
+        weight_sum = weight_sum + fold(jnp.where(inside, weight * weight, 0.0))
+        update_sum = update_sum + fold(jnp.where(inside, step * step, 0.0))
+        return weight_sum, update_sum
+
+    def pack(s, weight_sum, update_sum):
+        weight_sum = jnp.sum(jnp.sum(weight_sum, axis=0, keepdims=True), axis=1, keepdims=True)
+        update_sum = jnp.sum(jnp.sum(update_sum, axis=0, keepdims=True), axis=1, keepdims=True)
+        return jnp.where(lane == s, weight_sum, 0.0) + jnp.where(lane == SEGS + s, update_sum, 0.0)
+
     def segment(s, packed):
         begin, end = segment_span(seg, s, low, high)
         first_block = begin // BLOCK_ELEMS
         last_block = (end - 1) // BLOCK_ELEMS
 
         def edge(b, sums):
-            weight_sum, update_sum = sums
-            rows = pl.ds(pl.multiple_of(b * BLOCK, BLOCK), BLOCK)
-            place = element + b * BLOCK_ELEMS
-            inside = (place >= begin) & (place < end)
-            weight = w_own[rows, :]
-            step = u_own[rows, :]
-            weight_sum = weight_sum + fold(jnp.where(inside, weight * weight, 0.0))
-            update_sum = update_sum + fold(jnp.where(inside, step * step, 0.0))
-            return weight_sum, update_sum
+            return masked(b, sums, begin, end)
 
         def whole(group, sums):
             weight_sum, update_sum = sums
@@ -197,15 +211,21 @@
                 update_sum = update_sum + jnp.where(inner, update_sums[short, :], 0.0)
             return weight_sum, update_sum
 
-        zero = jnp.zeros((8, LANES), jnp.float32)
         sums = edge(first_block, (zero, zero))
         sums = lax.fori_loop((first_block + 1) // 8, (last_block + 7) // 8, whole, sums)
-        weight_sum, update_sum = lax.fori_loop(jnp.maximum(last_block, first_block + 1), last_block + 1, edge, sums)
-        weight_sum = jnp.sum(jnp.sum(weight_sum, axis=0, keepdims=True), axis=1, keepdims=True)
-        update_sum = jnp.sum(jnp.sum(update_sum, axis=0, keepdims=True), axis=1, keepdims=True)
-        return packed + jnp.where(lane == s, weight_sum, 0.0) + jnp.where(lane == SEGS + s, update_sum, 0.0)
-
-    packed = lax.fori_loop(first, last + 1, segment, jnp.zeros((8, LANES), jnp.float32))
+        sums = lax.fori_loop(jnp.maximum(last_block, first_block + 1), last_block + 1, edge, sums)
+        return packed + pack(s, *sums)
+
+    def one_tensor():
+        sums = live_sums
+        for b in range(LIVE, BLOCKS):
+            sums = masked(b, sums, 0, count)
+        return pack(first, *sums)
+
+    def several_tensors():
+        return lax.fori_loop(first, last + 1, segment, jnp.zeros((8, LANES), jnp.float32))
+
+    packed = lax.cond(first == last, one_tensor, several_tensors)
     for row in range(0, N_DP, 8):
         pay[pl.ds(row, 8), :] = packed
 
@@ -234,7 +254,8 @@
         for copy in body_copies:
             copy.start()
         sums = jnp.broadcast_to(jnp.sum(parts[...], axis=0, keepdims=True), (8, LANES))
-        rates = LEARN * jnp.sqrt(sums) / (jnp.sqrt(pltpu.roll(sums, SEGS, 1)) + EPSILON)
+        roots = jnp.sqrt(sums)
+        rates = LEARN * roots / (pltpu.roll(roots, SEGS, 1) + EPSILON)
 
         def rate_of(labels):
             pieces = [jnp.take_along_axis(rates, labels[r:r + 8], axis=1) for r in range(0, labels.shape[0], 8)]
@@ -334,7 +355,7 @@
         in_specs=[hbm] * 7,
         out_specs=[vmem] * 13,
         scratch_shapes=[state, state, pltpu.VMEM((ROWS, LANES), jnp.bfloat16), block_sums, block_sums,
-                        pltpu.VMEM((2 * SEGS, LANES), f32), bounds, bounds, starts,
+                        bounds, bounds, starts,
                         pltpu.SemaphoreType.DMA((4, 4)), pltpu.SemaphoreType.DMA((3,))],
         compiler_params=pltpu.CompilerParams(vmem_limit_bytes=24 * 2**20),
     )(*in_hbm(*flat, old_bounds, new_bounds, seg_start))

time: 26.7 us -> 26.6 us (level)
  no operation moved by 1% of the time
where the time goes in v6:
time: 26.6 us; the launch traced here: 26.4 us
  blocking collectives  12.4 us (47%)
  starting transfers between devices  8.86 us (33%)
  Pallas kernels  4.5 us (17%)
  between operations  0.64 us (2%)
    all_to_all x1, blocking collectives, shards(): parts = lax.all_to_all(pay, 'dp', 0, 0, tiled=True)  12.4 us
    ppermute x1, starting transfers between devices, shards(): from_core = lax.ppermute(send_core, 'dp', pairs)  6.47 us
    pallas_call x1, Pallas kernels, shards(): pl.pallas_call(prepare, out_shape=(jax.ShapeDtypeStruct((N_DP, LANES), f3...  3.09 us
    ppermute x1, starting transfers between devices, shards(): from_next = lax.ppermute(send_next, 'dp', between)  2.39 us
    pallas_call x1, Pallas kernels, shards(): pl.pallas_call(finish, out_shape=(jax.ShapeDtypeStruct((ROWS, LANES), f32...  1.41 us
  transfers between devices with their start and end apart: 2, of which 0 were waited for; matrix products, arithmetic and copies ran while one was open for 0% of the time, Pallas kernels for 0%

profile of v6, /device:TPU:1, one launch (start us, length us, event | category | flops | bytes accessed | tf_op | source)
XLA Modules:
  0.0 26.4 jit_solution(3559222816330826591)
XLA Ops:
  0.6 3.1 %shard_map.94 = (f32[128,128]{1,0:T(8,128)S(1)}, f32[1032,128]{1,0:T(8,128)S(1)}, f32[1032,128]{1,0:T(8,128)S(1)}, f32[1032,128]{1,0:T(8,128)S(1)}, f32[1032,128...) custom-call(f32[992,128]{1,0:T(8,128)} %bitcast.13, ...), custom_call_target="tpu_custom_call" | custom-call | tf_op jit(solution)/shard_map/pallas_call | solution.py:351
  3.7 2.4 %collective-permute-start = (f32[4,32,128]{2,1,0:T(8,128)S(1)}, f32[4,32,128]{2,1,0:T(8,128)S(1)}, u32[]{:S(2)}, u32[]{:S(2)}) collective-permute-start(f32[4,32,128]{2,1,0:T(8,128)S(1)} %get-tuple-element.24), channel_id=1, source_target_pairs={{0,127},{1,2},{2,1},{3,4},{4,3},{5,6},{6,5},{7,8},{8,7},{9,10},{10... | collective-permute-start | bytes 196616 | tf_op jit(solution)/shard_map/ppermute | solution.py:364
  6.1 6.5 %collective-permute-start.1 = (f32[4,32,128]{2,1,0:T(8,128)S(1)}, f32[4,32,128]{2,1,0:T(8,128)S(1)}, u32[]{:S(2)}, u32[]{:S(2)}) collective-permute-start(f32[4,32,128]{2,1,0:T(8,128)S(1)} %get-tuple-element.25), channel_id=1, source_target_pairs={{0,1},{1,0},{2,3},{3,2},{4,5},{5,4},{6,7},{7,6},{8,9},{9,8},{10,11... | collective-permute-start | bytes 196616 | tf_op jit(solution)/shard_map/ppermute | solution.py:365
  12.6 12.4 %all_to_all.11 = f32[128,1,128]{2,1,0:T(1,128)S(1)} all-to-all(f32[128,1,128]{2,1,0:T(1,128)S(1)} %bitcast.12), channel_id=1, replica_groups=mesh['dp'=128] {'dp'}, dimensions={0} | all-to-all | bytes 131072 | tf_op jit(solution)/shard_map/all_to_all | solution.py:366
  25.0 0.0 collective-permute-done.from_next
  25.0 0.0 collective-permute-done.1.from_core
  25.0 1.4 %shard_map.95 = (f32[992,128]{1,0:T(8,128)}, f32[992,128]{1,0:T(8,128)}, f32[992,128]{1,0:T(8,128)}) custom-call(f32[128,128]{1,0:T(8,128)S(1)} %bitcast.11, f32[1032,128]{1,0:T(8,128)S(1)} %get-tuple-element.20.w_own, f32[1032,128]{1,0:T(8,128)S(1)} %get-tuple-element.21.m_own, f32[1032,128]{1,0:T(8,128)S(1)} %get-tuple-element.22.v_own, ...), custom_call_target="tpu_custom_call" | custom-call | tf_op jit(solution)/shard_map/pallas_call | solution.py:367
Async XLA Ops:
  3.7 21.3 %collective-permute-start = (f32[4,32,128]{2,1,0:T(8,128)S(1)}, f32[4,32,128]{2,1,0:T(8,128)S(1)}, u32[]{:S(2)}, u32[]{:S(2)}) collective-permute-start(f32[4,32,128]{2,1,0:T(8,128)S(1)} %get-tuple-element.24), channel_id=1, source_target_pairs={{0,127},{1,2},{2,1},{3,4},{4,3},{5,6},{6,5},{7,8},{8,7},{9,10},{10... | collective-permute-start | bytes 196616 | tf_op jit(solution)/shard_map/ppermute | solution.py:364
  6.1 18.9 %collective-permute-start.1 = (f32[4,32,128]{2,1,0:T(8,128)S(1)}, f32[4,32,128]{2,1,0:T(8,128)S(1)}, u32[]{:S(2)}, u32[]{:S(2)}) collective-permute-start(f32[4,32,128]{2,1,0:T(8,128)S(1)} %get-tuple-element.25), channel_id=1, source_target_pairs={{0,1},{1,0},{2,3},{3,2},{4,5},{5,4},{6,7},{7,6},{8,9},{9,8},{10,11... | collective-permute-start | bytes 196616 | tf_op jit(solution)/shard_map/ppermute | solution.py:365

commit v7 on v6

--- a/solution.py
+++ b/solution.py
@@ -14,7 +14,7 @@
 PAD_ROWS = 1032
 TAIL = 896
 TAIL_ROWS = ROWS - TAIL
-BODY_PIECES = ((1, 14), (14, 22), (22, 28))
+BODY_PIECES = ((1, 8), (8, 15), (15, 22), (22, 28))
 
 BETA_ONE = 0.9
 BETA_TWO = 0.999
@@ -371,7 +371,7 @@
         out_specs=[hbm] * 3,
         scratch_shapes=[state] * 4 + [pltpu.VMEM((ROWS, LANES), jnp.int32), state]
         + [pltpu.VMEM((4, 136, LANES), f32), pltpu.VMEM((4, 136, LANES), f32), pltpu.VMEM((4, 48, LANES), f32),
-           starts, pltpu.SemaphoreType.DMA((12,)), pltpu.SemaphoreType.DMA],
+           starts, pltpu.SemaphoreType.DMA((13,)), pltpu.SemaphoreType.DMA],
         compiler_params=pltpu.CompilerParams(vmem_limit_bytes=24 * 2**20),
     )(parts, w_own, m_own, v_own, u_own, from_next, from_core, *early, *in_hbm(seg_start))
     return tuple(x.reshape(-1) for x in outs)

time: 26.6 us -> 26.7 us (level)
  no operation moved by 1% of the time
where the time goes in v7:
time: 26.7 us; the launch traced here: 26.5 us
  blocking collectives  12.4 us (46%)
  starting transfers between devices  8.98 us (34%)
  Pallas kernels  4.51 us (17%)
  between operations  0.64 us (2%)
    all_to_all x1, blocking collectives, shards(): parts = lax.all_to_all(pay, 'dp', 0, 0, tiled=True)  12.4 us
    ppermute x1, starting transfers between devices, shards(): from_core = lax.ppermute(send_core, 'dp', pairs)  6.58 us
    pallas_call x1, Pallas kernels, shards(): pl.pallas_call(prepare, out_shape=(jax.ShapeDtypeStruct((N_DP, LANES), f3...  3.09 us
    ppermute x1, starting transfers between devices, shards(): from_next = lax.ppermute(send_next, 'dp', between)  2.39 us
    pallas_call x1, Pallas kernels, shards(): pl.pallas_call(finish, out_shape=(jax.ShapeDtypeStruct((ROWS, LANES), f32...  1.42 us
  transfers between devices with their start and end apart: 2, of which 0 were waited for; matrix products, arithmetic and copies ran while one was open for 0% of the time, Pallas kernels for 0%

profile of v7, /device:TPU:1, one launch (start us, length us, event | category | flops | bytes accessed | tf_op | source)
XLA Modules:
  0.0 26.5 jit_solution(12780068719283579048)
XLA Ops:
  0.6 3.1 %shard_map.94 = (f32[128,128]{1,0:T(8,128)S(1)}, f32[1032,128]{1,0:T(8,128)S(1)}, f32[1032,128]{1,0:T(8,128)S(1)}, f32[1032,128]{1,0:T(8,128)S(1)}, f32[1032,128...) custom-call(f32[992,128]{1,0:T(8,128)} %bitcast.13, ...), custom_call_target="tpu_custom_call" | custom-call | tf_op jit(solution)/shard_map/pallas_call | solution.py:351
  3.7 2.4 %collective-permute-start = (f32[4,32,128]{2,1,0:T(8,128)S(1)}, f32[4,32,128]{2,1,0:T(8,128)S(1)}, u32[]{:S(2)}, u32[]{:S(2)}) collective-permute-start(f32[4,32,128]{2,1,0:T(8,128)S(1)} %get-tuple-element.24), channel_id=1, source_target_pairs={{0,127},{1,2},{2,1},{3,4},{4,3},{5,6},{6,5},{7,8},{8,7},{9,10},{10... | collective-permute-start | bytes 196616 | tf_op jit(solution)/shard_map/ppermute | solution.py:364
  6.1 6.6 %collective-permute-start.1 = (f32[4,32,128]{2,1,0:T(8,128)S(1)}, f32[4,32,128]{2,1,0:T(8,128)S(1)}, u32[]{:S(2)}, u32[]{:S(2)}) collective-permute-start(f32[4,32,128]{2,1,0:T(8,128)S(1)} %get-tuple-element.25), channel_id=1, source_target_pairs={{0,1},{1,0},{2,3},{3,2},{4,5},{5,4},{6,7},{7,6},{8,9},{9,8},{10,11... | collective-permute-start | bytes 196616 | tf_op jit(solution)/shard_map/ppermute | solution.py:365
  12.7 12.4 %all_to_all.11 = f32[128,1,128]{2,1,0:T(1,128)S(1)} all-to-all(f32[128,1,128]{2,1,0:T(1,128)S(1)} %bitcast.12), channel_id=1, replica_groups=mesh['dp'=128] {'dp'}, dimensions={0} | all-to-all | bytes 131072 | tf_op jit(solution)/shard_map/all_to_all | solution.py:366
  25.1 0.0 collective-permute-done.from_next
  25.1 0.0 collective-permute-done.1.from_core
  25.1 1.4 %shard_map.95 = (f32[992,128]{1,0:T(8,128)}, f32[992,128]{1,0:T(8,128)}, f32[992,128]{1,0:T(8,128)}) custom-call(f32[128,128]{1,0:T(8,128)S(1)} %bitcast.11, f32[1032,128]{1,0:T(8,128)S(1)} %get-tuple-element.20.w_own, f32[1032,128]{1,0:T(8,128)S(1)} %get-tuple-element.21.m_own, f32[1032,128]{1,0:T(8,128)S(1)} %get-tuple-element.22.v_own, ...), custom_call_target="tpu_custom_call" | custom-call | tf_op jit(solution)/shard_map/pallas_call | solution.py:367
Async XLA Ops:
  3.7 21.4 %collective-permute-start = (f32[4,32,128]{2,1,0:T(8,128)S(1)}, f32[4,32,128]{2,1,0:T(8,128)S(1)}, u32[]{:S(2)}, u32[]{:S(2)}) collective-permute-start(f32[4,32,128]{2,1,0:T(8,128)S(1)} %get-tuple-element.24), channel_id=1, source_target_pairs={{0,127},{1,2},{2,1},{3,4},{4,3},{5,6},{6,5},{7,8},{8,7},{9,10},{10... | collective-permute-start | bytes 196616 | tf_op jit(solution)/shard_map/ppermute | solution.py:364
  6.1 19.0 %collective-permute-start.1 = (f32[4,32,128]{2,1,0:T(8,128)S(1)}, f32[4,32,128]{2,1,0:T(8,128)S(1)}, u32[]{:S(2)}, u32[]{:S(2)}) collective-permute-start(f32[4,32,128]{2,1,0:T(8,128)S(1)} %get-tuple-element.25), channel_id=1, source_target_pairs={{0,1},{1,0},{2,3},{3,2},{4,5},{5,4},{6,7},{7,6},{8,9},{9,8},{10,11... | collective-permute-start | bytes 196616 | tf_op jit(solution)/shard_map/ppermute | solution.py:365
